TPU v7x, 256 devices: a whole 4x4x8 slice. The times are simulated.
256 devices in a mesh: expert: 4 (over z_lo, core), fsdp: 64 (over x, y, z_hi).
Axes of the slice: x: 4, y: 4, z: 8 (z_hi: 4, z_lo: 2; z = z_hi * 2 + z_lo), core: 2. Of those that a mesh axis runs over, the one named last changes fastest.
Arguments:
- tokens: bfloat16 [512, 4096], P(('expert', 'fsdp')), may hold values from -6 to 6
- routes: int32 [512, 2], P(('expert', 'fsdp')), may hold values from 0 to 3, all different within a row; in each aligned block of 2 rows (0 to 1, 2 to 3, ...) at most 2 rows name the same one
- gates: float32 [512, 2], P(('expert', 'fsdp')), may hold values from 0.2 to 1
- out_grad: bfloat16 [512, 4096], P(('expert', 'fsdp')), may hold values from -6 to 6
- gate_weight: bfloat16 [4, 4096, 16384], P('expert', None, 'fsdp'), may hold values from -0.09375 to 0.09375
- up_weight: bfloat16 [4, 4096, 16384], P('expert', None, 'fsdp'), may hold values from -0.09375 to 0.09375
- down_weight: bfloat16 [4, 16384, 4096], P('expert', 'fsdp'), may hold values from -0.046875 to 0.046875
Outputs:
- tokens_grad: bfloat16 [512, 4096], P(('expert', 'fsdp'))
- gate_weight_grad: bfloat16 [4, 4096, 16384], P('expert', None, 'fsdp')
- up_weight_grad: bfloat16 [4, 4096, 16384], P('expert', None, 'fsdp')
- down_weight_grad: bfloat16 [4, 16384, 4096], P('expert', 'fsdp')
Inputs may be any that keep to these rules, and one draw needn't show every extreme that they name: `routes`: each token names two different experts. The 2 tokens of one device name one expert at most 2 times, and in every draw some device's tokens name some expert exactly 2 times.
All inputs are finite; a program needn't handle non-finite values.
Results may differ from a plain program's by a relative error of at most 0.0066.
Values may be sent and summed in bfloat16 or wider, within the bound.
A program may use at most 128 MiB of HBM per device.

v0:
```python
import jax
import jax.numpy as jnp
from jax import lax
from jax.sharding import PartitionSpec as P

MOST = 2


def contract(left_side, right_side, left_dim, right_dim):
    return lax.dot_general(
        left_side,
        right_side,
        (((left_dim,), (right_dim,)), ((), ())),
        preferred_element_type=jnp.float32,
    )


def expert_rows(rows_x, rows_dy, w_gate, w_up, w_down):
    gate_act = jnp.dot(rows_x, w_gate, preferred_element_type=jnp.float32)
    up_act = jnp.dot(rows_x, w_up, preferred_element_type=jnp.float32)
    sigmoid_gate = jax.nn.sigmoid(gate_act)
    silu_gate = gate_act * sigmoid_gate
    hidden = (silu_gate * up_act).astype(jnp.bfloat16)
    hidden_grad = contract(rows_dy, w_down, 1, 1)
    gate_grad = (
        hidden_grad * up_act * sigmoid_gate * (1.0 + gate_act * (1.0 - sigmoid_gate))
    ).astype(jnp.bfloat16)
    up_grad = (hidden_grad * silu_gate).astype(jnp.bfloat16)
    return (hidden, gate_grad, up_grad)


def per_device(tokens, routes, gates, out_grad, gate_weight, up_weight, down_weight):
    tok_rows = tokens.shape[0]
    model_width = tokens.shape[1]
    groups = lax.axis_size("expert")
    slot_count = groups * MOST
    flat_routes = routes.reshape(-1)
    expert_ids = jnp.arange(groups, dtype=jnp.int32)
    onehot = (flat_routes[:, None] == expert_ids[None, :]).astype(jnp.int32)
    earlier = jnp.cumsum(onehot, axis=0) - onehot
    slot_of = jnp.sum(earlier * onehot, axis=1)
    target = flat_routes * MOST + slot_of
    placing = (jnp.arange(slot_count, dtype=jnp.int32)[:, None] == target[None, :]).astype(
        jnp.bfloat16
    )
    combine = jnp.sum(placing.reshape(slot_count, tok_rows, 2), axis=2)
    contrib = (gates[:, :, None] * out_grad[:, None, :].astype(jnp.float32)).astype(jnp.bfloat16)
    contrib = contrib.reshape(tok_rows * 2, model_width)
    send_x = jnp.dot(combine, tokens, preferred_element_type=jnp.float32).astype(jnp.bfloat16)
    send_dy = jnp.dot(placing, contrib, preferred_element_type=jnp.float32).astype(jnp.bfloat16)
    send_live = jnp.sum(combine, axis=1)
    recv_x, recv_dy, recv_live = (
        lax.all_to_all(send_x, "expert", split_axis=0, concat_axis=0, tiled=True),
        lax.all_to_all(send_dy, "expert", split_axis=0, concat_axis=0, tiled=True),
        lax.all_to_all(send_live, "expert", split_axis=0, concat_axis=0, tiled=True),
    )
    w_gate = gate_weight[0]
    w_up = up_weight[0]
    w_down = down_weight[0]
    group_x, group_dy, live_flag = (
        lax.all_gather(recv_x, "fsdp", axis=0, tiled=True),
        lax.all_gather(recv_dy, "fsdp", axis=0, tiled=True),
        lax.all_gather(recv_live, "fsdp", axis=0, tiled=True),
    )
    hidden, gate_rows, up_rows = expert_rows(group_x, group_dy, w_gate, w_up, w_down)
    gate_rows = gate_rows * live_flag[:, None]
    up_rows = up_rows * live_flag[:, None]
    grad_gate = contract(group_x, gate_rows, 0, 0)
    grad_up = contract(group_x, up_rows, 0, 0)
    grad_down = contract(hidden, group_dy, 0, 0)
    row_grad = lax.psum_scatter(
        contract(gate_rows, w_gate, 1, 1) + contract(up_rows, w_up, 1, 1),
        "fsdp",
        scatter_dimension=0,
        tiled=True,
    ).astype(jnp.bfloat16)
    returned = lax.all_to_all(row_grad, "expert", split_axis=0, concat_axis=0, tiled=True)
    tokens_grad = contract(combine, returned, 0, 0).astype(jnp.bfloat16)
    return (
        tokens_grad,
        grad_gate.astype(jnp.bfloat16)[None],
        grad_up.astype(jnp.bfloat16)[None],
        grad_down.astype(jnp.bfloat16)[None],
    )


def solution(mesh):
    return jax.shard_map(
        per_device,
        mesh=mesh,
        in_specs=(
            P(("expert", "fsdp"), None),
            P(("expert", "fsdp"), None),
            P(("expert", "fsdp"), None),
            P(("expert", "fsdp"), None),
            P("expert", None, "fsdp"),
            P("expert", None, "fsdp"),
            P("expert", "fsdp", None),
        ),
        out_specs=(
            P(("expert", "fsdp"), None),
            P("expert", None, "fsdp"),
            P("expert", None, "fsdp"),
            P("expert", "fsdp", None),
        ),
        check_vma=False,
    )
```

profile of v0, /device:TPU:1, one launch (start us, length us, event | category | flops | bytes accessed | tf_op | source)
XLA Modules:
  0.0 667.4 jit_solution(12262215140153729849)
XLA Ops:
  7.2 0.0 copy-start
  7.2 0.0 all-gather.5.cloned.1.call-start
  7.2 0.9 eq.36
  8.1 0.1 fusion.18
  8.2 0.2 select_reduce_fusion
  8.4 0.1 reduce_sum.36
  8.5 0.7 multiply_add_fusion
  9.2 0.1 fusion.19
  9.3 0.9 convolution_convert_fusion.3
  10.2 0.1 all_to_all.35
  10.3 8.9 %all_to_all.49 = bf16[4,2,4096]{2,1,0:T(2,128)(2,1)S(1)} all-to-all(bf16[4,2,4096]{2,1,0:T(2,128)(2,1)S(1)} %all_to_all.35), channel_id=1, replica_groups=mesh['expert'=4,'fsdp'=64] {'expert'}, dimensions={0} | all-to-all | bytes 131072 | tf_op jit(solution)/shard_map/all_to_all | solution.py:53
  19.1 0.7 all_to_all.37
  19.8 0.0 all-gather.5.cloned.1.call-update
  19.8 0.0 all-gather.3.cloned.1.call-start
  19.9 0.8 mul.69
  20.6 0.7 mul.71
  21.4 0.1 mul.72
  21.5 0.2 convolution_convert_fusion.4
  21.7 0.1 all_to_all.32
  21.7 6.5 all_to_all.50
  28.2 0.7 all_to_all.34
  28.9 0.0 all-gather.3.cloned.1.call-update
  28.9 0.7 all_to_all.44
  29.6 4.1 all-to-all-start.2
  33.6 1.3 dynamic-slice
  35.5 1.1 all-to-all-done.2
  36.6 0.1 reshape.44
  36.7 0.2 dynamic-update-slice
  36.9 177.6 %all-reduce = bf16[512]{0:T(512)(128)(2,1)S(1)} all-reduce(bf16[512]{0:T(512)(128)(2,1)S(1)} %dynamic-update-slice), channel_id=1, replica_groups=mesh['expert'=4,'fsdp'=64] {'fsdp'}, use_global_device_ids=true, to_apply=%add | all-reduce | flops 512 | bytes 2048
  214.5 0.0 all-gather.5.cloned.1.call-done
  214.5 0.0 copy-start.1
  214.6 3.6 fusion.5
  218.2 0.5 copy-done.3
  218.6 2.0 fusion.8
  220.7 4.3 fusion.13
  225.0 0.0 copy-start.2
  225.0 1.3 fusion.3
  226.3 0.3 copy-done.2
  226.6 4.6 convolution_add_fusion
  231.2 0.0 reduce-scatter.2.cloned.1.call-update
  231.2 5.0 fusion.1
  236.2 2.7 fusion.2
  238.9 365.6 %reduce-scatter.2.cloned.1.call-done = f32[8,4096]{1,0:T(8,128)} async-done(((f32[512,4096]{1,0:T(8,128)}), f32[8,4096]{1,0:T(8,128)}) %reduce-scatter.2.cloned.1.call-update) | async-done | bytes 131088 | tf_op jit(solution)/shard_map/reduce_scatter | solution.py:71
  604.5 0.9 convert_element_type.57
  605.4 0.7 all_to_all.41
  606.1 49.2 %all-to-all-start.3 = ((bf16[4,2,4096]{2,1,0:T(2,128)(2,1)}), bf16[4,2,4096]{2,1,0:T(2,128)(2,1)S(1)}, u32[]{:S(2)}, u32[]{:S(2)}) async-start(bf16[4,2,4096]{2,1,0:T(2,128)(2,1)} %all_to_all.41), calls=%async_computation.4 | async-start | bytes 131072 | tf_op jit(solution)/shard_map/all_to_all | solution.py:77
  655.3 4.8 fusion
  660.1 0.8 convolution_convert_fusion.5
  (15 shorter events, 0.1 us)
Async XLA Ops:
  7.2 207.4 %copy-start = (bf16[1,4096,256]{2,1,0:T(8,128)(2,1)S(1)}, bf16[1,4096,256]{2,1,0:T(8,128)(2,1)}, u32[]{:S(2)}) copy-start(bf16[1,4096,256]{2,1,0:T(8,128)(2,1)} %param.11) | copy-start | bytes 6291460
  7.2 207.3 %all-gather.5.cloned.1.call-start = ((), (), s32[]{:S(2)}) async-start(), calls=%async_computation.6 | async-start | bytes 4259840 | tf_op jit(solution)/shard_map/all_gather | solution.py:61
  19.8 200.8 %all-gather.3.cloned.1.call-start = ((), (), s32[]{:S(2)}) async-start(), calls=%async_computation.5 | async-start | bytes 4259840 | tf_op jit(solution)/shard_map/all_gather | solution.py:62
  29.6 7.0 %all-to-all-start.2 = ((bf16[4,2,1]{1,2,0:T(2,128)(2,1)}), bf16[4,2,1]{1,2,0:T(2,128)(2,1)S(1)}, u32[]{:S(2)}, u32[]{:S(2)}) async-start(bf16[4,2,1]{1,2,0:T(2,128)(2,1)} %all_to_all.44), calls=%async_computation.2 | async-start | bytes 4096 | tf_op jit(solution)/shard_map/all_to_all | solution.py:55
  33.6 570.9 %reduce-scatter.2.cloned.1.call-start = ((), (), s32[]{:S(2)}) async-start(), calls=%async_computation.7 | async-start | bytes 8519680 | tf_op jit(solution)/shard_map/reduce_scatter | solution.py:71
  214.5 3.6 copy-start.1
  214.5 4.1 copy-start.3
  225.0 1.6 copy-start.2
  231.2 5.0 copy-start.4
  231.2 5.0 copy-start.5
  606.1 54.0 %all-to-all-start.3 = ((bf16[4,2,4096]{2,1,0:T(2,128)(2,1)}), bf16[4,2,4096]{2,1,0:T(2,128)(2,1)S(1)}, u32[]{:S(2)}, u32[]{:S(2)}) async-start(bf16[4,2,4096]{2,1,0:T(2,128)(2,1)} %all_to_all.41), calls=%async_computation.4 | async-start | bytes 131072 | tf_op jit(solution)/shard_map/all_to_all | solution.py:77
Sparse Core Ops, SparseCore 0:
  19.9 91.5 all-gather.4
  115.5 88.0 all-gather.2
  231.3 373.0 reduce-scatter.1
where the time goes:
time: 668 us; the launch traced here: 667 us
  waiting for transfers between devices  367 us (55%)
  blocking collectives  193 us (29%)
  starting transfers between devices  53.4 us (8%)
  matrix products  30.2 us (5%)
  between operations  14.5 us (2%)
  local copies, waits for them, and re-layouts  7.69 us (1%)
    reduce_scatter x1, waiting for transfers between devices, per_device(): lax.psum_scatter(contract(gate_rows, w_gate, 1, 1) + contract(up_rows, w_...  366 us
    unnamed x1, blocking collectives  178 us
    all_to_all x1, starting transfers between devices, per_device(): lax.all_to_all(row_grad, 'expert', split_axis=0, concat_axis=0, tiled=True)  49.2 us
    dot_general x7, matrix products, contract(): lax.dot_general(left_side, right_side, (((left_dim,), (right_dim,)), ((),...  23.5 us
  transfers between devices with their start and end apart: 5, of which 2 were waited for; matrix products, arithmetic and copies ran while one was open for 3% of the time, Pallas kernels for 0%

commit v1 on v0

v1 whole, which is shorter than its diff:
```python
import functools

import jax
import jax.numpy as jnp
from jax import lax
from jax.experimental import pallas as pl
from jax.experimental.pallas import tpu as pltpu
from jax.sharding import PartitionSpec as P

MESH = pl.DeviceIdType.MESH
BF = jnp.bfloat16
F32 = jnp.float32
D = 4096
SL = 128
CB = 8 * SL
W = D + 128
CA = W - CB
HW = D // 2


def gather_kernel(p_ref, big, stk, zbuf, blk, s1, r1, sp, rp, sa, ra, sb, rb, sf, rf, szp, rzp, szm, rzm, ssib, rsib):
    e=lax.axis_index("expert"); f=lax.axis_index("fsdp")
    c=e%2; zl=e//2; zh=f%4; z=zh*2+zl; x=f//16; y=(f//4)%4
    c0=1-c
    i1=y*c0+x*c; i2=x*c0+y*c
    st1=4*c0+16*c; st2=16*c0+4*c
    def dv(a,b): return {"expert":e,"fsdp":(a%4)*st1+(b%4)*st2+zh}
    def bj(a,b): return ((a%4)*st1+(b%4)*st2)//4
    def dz(zz,cc): return {"expert":(zz%2)*2+cc,"fsdp":(f//4)*4+zz//2}
    def rc(src,dst,ss,rs,d):
        return pltpu.make_async_remote_copy(src_ref=src,dst_ref=dst,send_sem=ss,recv_sem=rs,device_id=d,device_id_type=MESH)
    bar=pltpu.get_barrier_semaphore()
    zoff=[(dd,cc) for dd in range(8) for cc in range(2) if (dd,cc)!=(0,0)]
    poff=[(a,b) for a in range(4) for b in range(4) if (a,b)!=(0,0)]
    for dd,cc in zoff: pl.semaphore_signal(bar,inc=1,device_id=dz((z+dd)%8,(c+cc)%2),device_id_type=MESH)
    for a,b in poff: pl.semaphore_signal(bar,inc=1,device_id=dv(i1+a,i2+b),device_id_type=MESH)
    stk[...]=p_ref[...]
    pl.semaphore_wait(bar,30)
    me=z*2+c
    c1=[]
    order=sorted(range(15),key=lambda i:-min(zoff[i][0],8-zoff[i][0]))
    for i in order:
        dd,cc=zoff[i]
        cp=rc(stk.at[(c+cc)%2],zbuf.at[me],s1.at[i],r1.at[i],dz((z+dd)%8,(c+cc)%2)); cp.start(); c1.append(cp)
    zbuf[me]=stk[c]
    for i in reversed(order):
        dd,cc=zoff[i]
        src=((z+8-dd)%8)*2+(c+cc)%2
        rc(stk.at[0],zbuf.at[src],s1.at[i],r1.at[i],dz(0,0)).wait_recv()
    for i in range(16):
        blk[2*i:2*i+2,:]=zbuf[i].astype(F32)
    jo=bj(i1,i2)
    big[c,jo,:,CB:W]=blk[:,CB:W].astype(BF)
    mycol=pl.ds(pl.multiple_of(SL*z,128),SL)
    big[c,jo,:,mycol]=blk[:,mycol].astype(BF)
    for cp in c1: cp.wait_send()
    sends=[]
    for i,(a,b) in enumerate(poff):
        cp=rc(big.at[c,jo,:,mycol],big.at[c,jo,:,mycol],sp.at[i],rp.at[i],dv(i1+a,i2+b)); cp.start(); sends.append(cp)
    A=lambda j: big.at[c,j,:,CB:W]
    def a2send(k,a):
        j=bj(i1+a,i2)
        for t,s in ((0,1),(1,-1)):
            cp=rc(A(j),A(j),sb.at[2*k+t],rb.at[2*k+t],dv(i1,i2+s)); cp.start(); sends.append(cp)
    for a in (1,3,2):
        cp=rc(A(jo),A(jo),sa.at[a-1],ra.at[a-1],dv(i1+a,i2)); cp.start(); sends.append(cp)
    a2send(0,0)
    sibn=[0]
    sib={"expert":zl*2+c0,"fsdp":f}
    sibw=[]
    def sibsend(ref, oref):
        i=sibn[0]; sibn[0]+=1
        cp=rc(ref,ref,ssib.at[i],rsib.at[i],sib); cp.start(); sends.append(cp)
        sibw.append((oref,i))
    o_i1=i2; o_i2=i1
    def obj(a,b): return ((a%4)*st2+(b%4)*st1)//4
    def AO(j): return big.at[c0,j,:,CB:W]
    sibsend(A(jo),AO(obj(o_i1,o_i2)))
    for i,(a,b) in enumerate(poff):
        j=bj(i1-a+4,i2-b+4)
        rc(big.at[c,jo,:,mycol],big.at[c,j,:,mycol],sp.at[i],rp.at[i],dv(0,0)).wait_recv()
    def zc(k): return pl.ds(pl.multiple_of(SL*((z+k+8)%8),128),SL)
    S=lambda k: big.at[c,:,:,zc(k)]
    SO=lambda k: big.at[c0,:,:,zc(k)]
    H=lambda k,h: big.at[c,8*h:8*h+8,:,zc(k)]
    def zsend(h):
        if h<3:
            cp=rc(S(-h),S(-h),szp.at[h],rzp.at[h],dz((z+1)%8,c)); cp.start(); sends.append(cp)
            cp=rc(S(h),S(h),szm.at[h],rzm.at[h],dz((z+7)%8,c)); cp.start(); sends.append(cp)
        else:
            cp=rc(H(-3,0),H(-3,0),szp.at[3],rzp.at[3],dz((z+1)%8,c)); cp.start(); sends.append(cp)
            cp=rc(H(3,1),H(3,1),szm.at[3],rzm.at[3],dz((z+7)%8,c)); cp.start(); sends.append(cp)
    def zrecv(h):
        if h<3:
            rc(S(0),S(-h-1),szp.at[h],rzp.at[h],dz(0,0)).wait_recv()
            rc(S(0),S(h+1),szm.at[h],rzm.at[h],dz(0,0)).wait_recv()
            sibsend(S(-h-1),SO(-h-1)); sibsend(S(h+1),SO(h+1))
        else:
            rc(H(0,0),H(-4,0),szp.at[3],rzp.at[3],dz(0,0)).wait_recv()
            rc(H(0,1),H(4,1),szm.at[3],rzm.at[3],dz(0,0)).wait_recv()
            sibsend(S(4),SO(4))
    zsend(0)
    sibsend(S(0),SO(0))
    for a in (1,3,2):
        j=bj(i1-a+4,i2)
        rc(A(jo),A(j),sa.at[a-1],ra.at[a-1],dv(0,0)).wait_recv()
        a2send(a,4-a)
        sibsend(A(j),AO(obj(o_i1-a+4,o_i2)))
    AH=lambda j,h: big.at[c,j,16*h:16*h+16,CB:W]
    def a2recv(k,a):
        jm=bj(i1+a,i2+3); jp=bj(i1+a,i2+1)
        rc(A(jo),A(jm),sb.at[2*k],rb.at[2*k],dv(0,0)).wait_recv()
        cp=rc(AH(jm,0),AH(jm,0),sf.at[2*k],rf.at[2*k],dv(i1,i2+1)); cp.start(); sends.append(cp)
        rc(A(jo),A(jp),sb.at[2*k+1],rb.at[2*k+1],dv(0,0)).wait_recv()
        cp=rc(AH(jp,1),AH(jp,1),sf.at[2*k+1],rf.at[2*k+1],dv(i1,i2+3)); cp.start(); sends.append(cp)
        sibsend(A(jm),AO(obj(o_i1+a,o_i2+3)))
        sibsend(A(jp),AO(obj(o_i1+a,o_i2+1)))
    def a2fin(k,a):
        j=bj(i1+a,i2+2)
        rc(AH(jo,0),AH(j,0),sf.at[2*k],rf.at[2*k],dv(0,0)).wait_recv()
        rc(AH(jo,1),AH(j,1),sf.at[2*k+1],rf.at[2*k+1],dv(0,0)).wait_recv()
        sibsend(A(j),AO(obj(o_i1+a,o_i2+2)))
    ks=[(0,0),(1,3),(3,1),(2,2)]
    zrecv(0); zsend(1)
    a2recv(*ks[0])
    zrecv(1); zsend(2)
    a2recv(*ks[1])
    a2recv(*ks[2])
    zrecv(2); zsend(3)
    a2fin(*ks[0])
    a2recv(*ks[3])
    a2fin(*ks[1]); a2fin(*ks[2])
    zrecv(3)
    a2fin(*ks[3])
    for oref,i in sibw:
        rc(oref,oref,ssib.at[i],rsib.at[i],sib).wait_recv()
    for cp in sends: cp.wait_send()

def gather(payload):
    dma=pltpu.SemaphoreType.DMA
    return pl.pallas_call(gather_kernel,
        out_shape=jax.ShapeDtypeStruct((2,16,32,W),BF),
        in_specs=[pl.BlockSpec(memory_space=pltpu.VMEM)],out_specs=pl.BlockSpec(memory_space=pltpu.VMEM),
        scratch_shapes=[pltpu.VMEM((2,2,W),BF),pltpu.VMEM((16,2,W),BF),pltpu.VMEM((32,W),F32),
          dma((15,)),dma((15,)),dma((15,)),dma((15,)),dma((3,)),dma((3,)),dma((8,)),dma((8,)),dma((8,)),dma((8,)),dma((4,)),dma((4,)),dma((4,)),dma((4,)),dma((24,)),dma((24,))],
        compiler_params=pltpu.CompilerParams(collective_id=0,has_side_effects=True,vmem_limit_bytes=60<<20),name="gatherk")(payload)


def rs_kernel(pg, out, sbuf, acc0, r1, acc1, r2, acc2, zs, r3, ss0, rs0, ss1, rs1, ss2, rs2, ss3, rs3):
    e=lax.axis_index("expert"); f=lax.axis_index("fsdp")
    c=e%2; zl=e//2; zh=f%4; z=zh*2+zl; x=f//16; y=(f//4)%4
    c0=1-c
    i1=y*c0+x*c; i2=x*c0+y*c
    st1=4*c0+16*c; st2=16*c0+4*c
    def dv(a,b): return {"expert":e,"fsdp":(a%4)*st1+(b%4)*st2+zh}
    def bj(a,b): return ((a%4)*st1+(b%4)*st2)//4
    def dz(zz,cc): return {"expert":(zz%2)*2+cc,"fsdp":(f//4)*4+zz//2}
    def rc(src,dst,ss,rs,d):
        return pltpu.make_async_remote_copy(src_ref=src,dst_ref=dst,send_sem=ss,recv_sem=rs,device_id=d,device_id_type=MESH)
    bar=pltpu.get_barrier_semaphore()
    zoff=[(dd,cc) for dd in range(8) for cc in range(2) if (dd,cc)!=(0,0)]
    for dd,cc in zoff: pl.semaphore_signal(bar,inc=1,device_id=dz((z+dd)%8,(c+cc)%2),device_id_type=MESH)
    for a in (1,2,3):
        pl.semaphore_signal(bar,inc=1,device_id=dv(i1+a,i2),device_id_type=MESH)
        pl.semaphore_signal(bar,inc=1,device_id=dv(i1,i2+a),device_id_type=MESH)
    pl.semaphore_wait(bar,21)
    sib={"expert":zl*2+c0,"fsdp":f}
    mine=pl.ds(pl.multiple_of(c*HW,128),HW); other=pl.ds(pl.multiple_of(c0*HW,128),HW)
    sends=[]
    for j in range(16):
        cp=rc(pg.at[j,:,other],sbuf.at[j],ss0.at[j],rs0.at[j],sib); cp.start(); sends.append(cp)
    for j in range(16):
        rc(pg.at[j,:,other],sbuf.at[j],ss0.at[j],rs0.at[j],sib).wait_recv()
    def addj(j,_):
        acc0[j]=(pg[j,:,mine].astype(F32)+sbuf[j].astype(F32)).astype(BF)
        return 0
    for b in (2,1,3):
        for a in range(4):
            addj(bj(a,i2+b),0)
        for a in range(4):
            j=bj(a,i2+b)
            i=(b-1)*4+a
            cp=rc(acc0.at[j],r1.at[b-1,a],ss1.at[i],rs1.at[i],dv(i1,i2+b)); cp.start(); sends.append(cp)
    for b in (1,3,2):
        for a in range(4):
            i=(b-1)*4+a
            rc(acc0.at[0],r1.at[b-1,a],ss1.at[i],rs1.at[i],dv(0,0)).wait_recv()
    def sum1(a):
        j=bj(a,i2)
        ai=a%4
        return pg[j,:,mine].astype(F32)+sbuf[j].astype(F32)+r1[0,ai].astype(F32)+r1[1,ai].astype(F32)+r1[2,ai].astype(F32)
    for k,a in enumerate((2,1,3)):
        acc1[a-1]=sum1(i1+a).astype(BF)
        cp=rc(acc1.at[a-1],r2.at[a-1],ss2.at[a-1],rs2.at[a-1],dv(i1+a,i2)); cp.start(); sends.append(cp)
    acc2[...]=sum1(i1)
    for a in (1,3,2):
        rc(acc1.at[0],r2.at[a-1],ss2.at[a-1],rs2.at[a-1],dv(0,0)).wait_recv()
    acc2[...]=acc2[...]+r2[0].astype(F32)+r2[1].astype(F32)+r2[2].astype(F32)
    for i in range(16):
        zs[i]=acc2[2*i:2*i+2,:].astype(BF)
    order=sorted(range(15),key=lambda i:-min(zoff[i][0],8-zoff[i][0]))
    for i in order:
        dd,cc=zoff[i]
        t=((z+dd)%8)*2+(c+cc)%2
        cp=rc(zs.at[t],r3.at[z,c],ss3.at[i],rs3.at[i],dz((z+dd)%8,(c+cc)%2)); cp.start(); sends.append(cp)
    r3[z,c]=zs[z*2+c]
    for i in reversed(order):
        dd,cc=zoff[i]
        rc(zs.at[0],r3.at[(z+8-dd)%8,(c+cc)%2],ss3.at[i],rs3.at[i],dz(0,0)).wait_recv()
    for h in range(2):
        s=r3[0,h].astype(F32)
        for k in range(1,8): s=s+r3[k,h].astype(F32)
        out[:,h*HW:(h+1)*HW]=s.astype(BF)
    for cp in sends: cp.wait_send()

def rscat(pg,cid=1):
    dma=pltpu.SemaphoreType.DMA; V=pltpu.VMEM
    return pl.pallas_call(rs_kernel,
        out_shape=jax.ShapeDtypeStruct((2,4096),BF),
        in_specs=[pl.BlockSpec(memory_space=V)],out_specs=pl.BlockSpec(memory_space=V),
        scratch_shapes=[V((16,32,HW),BF),V((16,32,HW),BF),V((3,4,32,HW),BF),V((3,32,HW),BF),V((3,32,HW),BF),V((32,HW),F32),V((16,2,HW),BF),V((8,2,2,HW),BF),
          dma((16,)),dma((16,)),dma((12,)),dma((12,)),dma((3,)),dma((3,)),dma((15,)),dma((15,))],
        compiler_params=pltpu.CompilerParams(collective_id=cid,has_side_effects=True,vmem_limit_bytes=60<<20),name="rsk")(pg)


def contract(left, right, left_dim, right_dim):
    return lax.dot_general(left, right, (((left_dim,), (right_dim,)), ((), ())), preferred_element_type=F32)


def per_device(tokens, routes, gates, out_grad, gate_weight, up_weight, down_weight):
    expert_ids = jnp.arange(4, dtype=jnp.int32)
    dense = jnp.sum(jnp.where(routes[:, :, None] == expert_ids, gates[:, :, None], 0.0), axis=1)
    high = lax.reduce_precision(dense, 8, 7)
    middle = lax.reduce_precision(dense - high, 8, 7)
    low = dense - high - middle
    codes = jnp.concatenate([high, middle, low, jnp.zeros((2, 116), F32)], axis=1).astype(BF)
    payload = jnp.stack(
        [jnp.concatenate([tokens, codes], axis=1), jnp.concatenate([out_grad, codes], axis=1)]
    )
    big = gather(payload).reshape(2, 512, W)
    rows_x = big[0, :, :D]
    rows_dy = big[1, :, :D]
    e = lax.axis_index("expert")
    lane = jnp.arange(128, dtype=jnp.int32)
    own = (lane % 4 == e) & (lane < 12)
    gate = jnp.sum(jnp.where(own, big[1, :, D:].astype(F32), 0.0), axis=1, keepdims=True)
    w_gate = gate_weight[0]
    w_up = up_weight[0]
    w_down = down_weight[0]
    gate_act = contract(rows_x, w_gate, 1, 0)
    up_act = contract(rows_x, w_up, 1, 0)
    sigmoid_gate = jax.nn.sigmoid(gate_act)
    silu_gate = gate_act * sigmoid_gate
    hidden = (gate * (silu_gate * up_act)).astype(BF)
    hidden_grad = gate * contract(rows_dy, w_down, 1, 1)
    gate_grad = (hidden_grad * up_act * sigmoid_gate * (1.0 + gate_act * (1.0 - sigmoid_gate))).astype(BF)
    up_grad = (hidden_grad * silu_gate).astype(BF)
    partial = (contract(gate_grad, w_gate, 1, 1) + contract(up_grad, w_up, 1, 1)).astype(BF)
    tokens_grad = rscat(partial.reshape(16, 32, D))
    return (
        tokens_grad,
        contract(rows_x, gate_grad, 0, 0).astype(BF)[None],
        contract(rows_x, up_grad, 0, 0).astype(BF)[None],
        contract(hidden, rows_dy, 0, 0).astype(BF)[None],
    )


def solution(mesh):
    return jax.shard_map(
        per_device,
        mesh=mesh,
        in_specs=(
            P(("expert", "fsdp"), None),
            P(("expert", "fsdp"), None),
            P(("expert", "fsdp"), None),
            P(("expert", "fsdp"), None),
            P("expert", None, "fsdp"),
            P("expert", None, "fsdp"),
            P("expert", "fsdp", None),
        ),
        out_specs=(
            P(("expert", "fsdp"), None),
            P("expert", None, "fsdp"),
            P("expert", None, "fsdp"),
            P("expert", "fsdp", None),
        ),
        check_vma=False,
    )
```

time: 668 us -> 115 us (0.17)
  waiting for transfers between devices: 367 us -> 0 us
  blocking collectives: 193 us -> 0 us
  Pallas kernels: 0 us -> 86.4 us
  starting transfers between devices: 53.4 us -> 0 us
  between operations: 14.5 us -> 0.73 us
  matrix products: 30.2 us -> 20.4 us
    reduce_scatter x1 -> x0, waiting for transfers between devices: 366 us -> none  [per_device(): lax.psum_scatter(contract(gate_rows, w_gate, 1, 1) + contract(up_rows, w_...]
    unnamed x1 -> x0, blocking collectives: 178 us -> none
    pallas_call x0 -> x2, Pallas kernels: none -> 86.4 us  [the longest x1 50.7 us: gather(): pl.pallas_call(gather_kernel, out_shape=jax.ShapeDtypeStruct((2, 16, 32,...]
    all_to_all x2 -> x0, starting transfers between devices: 53.3 us -> none  [the longest x1 49.2 us: per_device(): lax.all_to_all(row_grad, 'expert', split_axis=0, concat_axis=0, tiled=True)]
    all_to_all x2 -> x0, blocking collectives: 15.3 us -> none  [the longest x1 8.86 us: per_device(): lax.all_to_all(send_x, 'expert', split_axis=0, concat_axis=0, tiled=True)]
    dot_general x11 -> x8, matrix products: 30.2 us -> 20.4 us  [contract(): lax.dot_general(left, right, (((left_dim,), (right_dim,)), ((), ())), pre...]
  transfers between devices with their start and end apart: 5 -> 0, of which waited for: 2 -> 0; matrix products, arithmetic and copies ran while one was open for 3% -> 0% of each run, Pallas kernels for 0% -> 0%
where the time goes in v1:
time: 115 us
  Pallas kernels  86.4 us (75%)
  matrix products  20.4 us (18%)
  local copies, waits for them, and re-layouts  4.39 us (4%)
  other arithmetic  2.63 us (2%)
    pallas_call x1, Pallas kernels, gather(): pl.pallas_call(gather_kernel, out_shape=jax.ShapeDtypeStruct((2, 16, 32,...  50.7 us
    pallas_call x1, Pallas kernels, rscat(): pl.pallas_call(rs_kernel, out_shape=jax.ShapeDtypeStruct((2, 4096), BF),...  35.7 us
    dot_general x8, matrix products, contract(): lax.dot_general(left, right, (((left_dim,), (right_dim,)), ((), ())), pre...  20.4 us
    unnamed x9, local copies, waits for them, and re-layouts  2.77 us

profile of v1, /device:TPU:1, one launch (start us, length us, event | category | flops | bytes accessed | tf_op | source)
XLA Modules:
  0.0 114.6 jit_solution(16035366934978111593)
XLA Ops:
  0.6 0.0 copy-start
  0.7 0.9 fusion.19
  1.6 0.8 concatenate.11
  2.4 0.8 concatenate.10
  3.2 0.7 pad_maximum_fusion.p_ref
  3.9 50.7 %gatherk.1 = bf16[2,16,32,4224]{3,2,1,0:T(8,128)(2,1)} custom-call(bf16[2,2,4224]{2,1,0:T(2,128)(2,1)} %pad_maximum_fusion.p_ref), custom_call_target="tpu_custom_call" | custom-call | tf_op jit(solution)/shard_map/gatherk/pallas_call | solution.py:141
  54.6 1.0 fusion.16
  55.6 0.0 copy-done
  55.6 0.0 copy-start.1
  55.6 3.6 %fusion.4 = f32[512,256]{1,0:T(8,128)S(1)} fusion(bf16[2,512,4224]{2,1,0:T(8,128)(2,1)} %bitcast.52, bf16[1,4096,256]{2,1,0:T(8,128)(2,1)S(1)} %copy-done), kind=kOutput, calls=%fused_computation.10 | convolution fusion | flops 1073741824 | bytes 6815744 | tf_op jit(solution)/shard_map/dot_general | solution.py:227
  59.2 1.1 copy-done.1
  60.3 0.0 copy-start.3
  60.3 3.0 %fusion.5 = f32[512,256]{1,0:T(8,128)S(1)} fusion(bf16[2,512,4224]{2,1,0:T(8,128)(2,1)S(1)} %bitcast.53, bf16[1,4096,256]{2,1,0:T(8,128)(2,1)} %param.12), kind=kOutput, calls=%fused_computation.11 | convolution fusion | flops 1073741824 | bytes 6815744 | tf_op jit(solution)/shard_map/dot_general | solution.py:227
  63.3 0.0 copy-done.3
  63.3 1.4 %multiply_convert_fusion.1 = (bf16[512,256]{1,0:T(8,128)(2,1)S(1)}, bf16[512,256]{1,0:T(8,128)(2,1)S(1)}) fusion(f32[512,256]{1,0:T(8,128)S(1)} %fusion.4, f32[512,256]{1,0:T(8,128)S(1)} %fusion.5, bf16[1,256,4096]{2,1,0:T(8,128)(2,1)S(1)} %copy-done.3, bf16[2,512,4224]{2,1,0:T(8,128)(2,1)S(1)} %bitcast.54, f32[512]{0:T(512)S(1)} %fusion.16), kind=kOutput, calls=%fused_computation.20 | convolution fusion | flops 1075576832 | bytes 7866368 | tf_op jit(solution)/shard_map/dot_general | solution.py:227
  64.7 2.7 %fusion.2 = bf16[1,256,4096]{2,1,0:T(8,128)(2,1)} fusion(bf16[2,512,4224]{2,1,0:T(8,128)(2,1)S(1)} %bitcast.55, f32[512,256]{1,0:T(8,128)S(1)} %fusion.5, f32[512]{0:T(512)S(1)} %fusion.16, f32[512,256]{1,0:T(8,128)S(1)} %fusion.4), kind=kOutput, calls=%fused_computation.6 | convolution fusion | flops 1075707904 | bytes 7342080 | tf_op jit(solution)/shard_map/dot_general | solution.py:227
  67.4 2.6 %fusion.1 = bf16[1,4096,256]{2,1,0:T(8,128)(2,1)} fusion(bf16[512,256]{1,0:T(8,128)(2,1)S(1)} %get-tuple-element.4, bf16[2,512,4224]{2,1,0:T(8,128)(2,1)S(1)} %bitcast.56), kind=kOutput, calls=%fused_computation.5 | convolution fusion | flops 1074790400 | bytes 6553600 | tf_op jit(solution)/shard_map/dot_general | solution.py:227
  70.0 2.6 %fusion = bf16[1,4096,256]{2,1,0:T(8,128)(2,1)} fusion(bf16[512,256]{1,0:T(8,128)(2,1)S(1)} %get-tuple-element.5, bf16[2,512,4224]{2,1,0:T(8,128)(2,1)S(1)} %bitcast.57), kind=kOutput, calls=%fused_computation.4 | convolution fusion | flops 1074790400 | bytes 6553600 | tf_op jit(solution)/shard_map/dot_general | solution.py:227
  72.7 0.0 copy-start.2
  72.7 1.3 %fusion.6 = f32[512,4096]{1,0:T(8,128)S(1)} fusion(bf16[512,256]{1,0:T(8,128)(2,1)S(1)} %get-tuple-element.5, bf16[1,4096,256]{2,1,0:T(8,128)(2,1)S(1)} %copy-done), kind=kOutput, calls=%fused_computation.12 | convolution fusion | flops 1073741824 | bytes 10747904 | tf_op jit(solution)/shard_map/dot_general | solution.py:227
  74.0 0.3 copy-done.2
  74.3 3.2 %add_convert_fusion = bf16[512,4096]{1,0:T(8,128)(2,1)} fusion(f32[512,4096]{1,0:T(8,128)S(1)} %fusion.6, bf16[512,256]{1,0:T(8,128)(2,1)S(1)} %get-tuple-element.4, bf16[1,4096,256]{2,1,0:T(8,128)(2,1)S(1)} %copy-done.2), kind=kOutput, calls=%fused_computation | convolution fusion | flops 1077936128 | bytes 14942208 | tf_op jit(solution)/shard_map/dot_general | solution.py:227
  77.5 35.7 %rsk.1 = bf16[2,4096]{1,0:T(2,128)(2,1)} custom-call(bf16[16,32,4096]{2,1,0:T(8,128)(2,1)} %bitcast.50), custom_call_target="tpu_custom_call" | custom-call | tf_op jit(solution)/shard_map/rsk/pallas_call | solution.py:218
  113.2 1.3 %copy.12 = bf16[2,4096]{1,0:T(2,128)(2,1)} copy(bf16[2,4096]{1,0:T(2,128)(2,1)} %rsk.1) | data formatting | bytes 32768
  (3 shorter events, 0.0 us)
Async XLA Ops:
  0.6 55.0 %copy-start = (bf16[1,4096,256]{2,1,0:T(8,128)(2,1)S(1)}, bf16[1,4096,256]{2,1,0:T(8,128)(2,1)}, u32[]{:S(2)}) copy-start(bf16[1,4096,256]{2,1,0:T(8,128)(2,1)} %param.11) | copy-start | bytes 6291460
  55.6 4.7 %copy-start.1 = (bf16[2,16,32,4224]{3,2,1,0:T(8,128)(2,1)S(1)}, bf16[2,16,32,4224]{3,2,1,0:T(8,128)(2,1)}, u32[]{:S(2)}) copy-start(bf16[2,16,32,4224]{3,2,1,0:T(8,128)(2,1)} %gatherk.1) | copy-start | bytes 25952260
  60.3 3.0 %copy-start.3 = (bf16[1,256,4096]{2,1,0:T(8,128)(2,1)S(1)}, bf16[1,256,4096]{2,1,0:T(8,128)(2,1)}, u32[]{:S(2)}) copy-start(bf16[1,256,4096]{2,1,0:T(8,128)(2,1)} %param.13) | copy-start | bytes 6291460
  72.7 1.6 %copy-start.2 = (bf16[1,4096,256]{2,1,0:T(8,128)(2,1)S(1)}, bf16[1,4096,256]{2,1,0:T(8,128)(2,1)}, u32[]{:S(2)}) copy-start(bf16[1,4096,256]{2,1,0:T(8,128)(2,1)} %param.12) | copy-start | bytes 6291460

commit v2 on v0

v2 whole, which is shorter than its diff:
```python
import jax
import jax.numpy as jnp
from jax import lax
from jax.experimental import pallas as pl
from jax.experimental.pallas import tpu as pltpu
from jax.sharding import PartitionSpec as P

MESH = pl.DeviceIdType.MESH
BF = jnp.bfloat16
F32 = jnp.float32
D = 4096
FB = 256
SL = 128
CB = 8 * SL
W = D + 128
HW = D // 2
QC = 512
NQ = HW // QC


def mm(left, right):
    return lax.dot_general(left, right, (((1,), (0,)), ((), ())), preferred_element_type=F32)


def mmt(left, right):
    return lax.dot_general(left, right, (((1,), (1,)), ((), ())), preferred_element_type=F32)


def main_kernel(
    tok_ref, route_ref, gate_ref, og_ref, wg_hbm, wu_hbm, wd_hbm,
    out, bigo, guo, hso,
    big, stk, zbuf, blk, wg, wu, wd, act_g, act_u, act_h, gu, hs,
    pgo, sbuf, acc, own1, r1, acc1, r2, own2, zs, r3,
    wsem, osem, s1, rv1, sp, rp, sa, ra, sb, rb, sf, rf, szp, rzp, szm, rzm, ssib, rsib,
    ss0, rs0, ss1, rs1, ss2, rs2, ss3, rs3,
):
    e = lax.axis_index("expert")
    f = lax.axis_index("fsdp")
    c = e % 2
    zl = e // 2
    zh = f % 4
    z = zh * 2 + zl
    x = f // 16
    y = (f // 4) % 4
    c0 = 1 - c
    i1 = y * c0 + x * c
    i2 = x * c0 + y * c
    st1 = 4 * c0 + 16 * c
    st2 = 16 * c0 + 4 * c

    def dv(a, b):
        return {"expert": e, "fsdp": (a % 4) * st1 + (b % 4) * st2 + zh}

    def bj(a, b):
        return ((a % 4) * st1 + (b % 4) * st2) // 4

    def obj(a, b):
        return ((a % 4) * st2 + (b % 4) * st1) // 4

    def dz(zz, cc):
        return {"expert": (zz % 2) * 2 + cc, "fsdp": (f // 4) * 4 + zz // 2}

    sib = {"expert": zl * 2 + c0, "fsdp": f}

    def rc(src, dst, ss, rs, d):
        return pltpu.make_async_remote_copy(
            src_ref=src, dst_ref=dst, send_sem=ss, recv_sem=rs, device_id=d, device_id_type=MESH
        )

    sends = []

    def go(*args):
        cp = rc(*args)
        cp.start()
        sends.append(cp)

    bar = pltpu.get_barrier_semaphore()
    zoff = [(dd, cc) for dd in range(8) for cc in range(2) if (dd, cc) != (0, 0)]
    poff = [(a, b) for a in range(4) for b in range(4) if (a, b) != (0, 0)]
    for dd, cc in zoff:
        pl.semaphore_signal(bar, inc=1, device_id=dz((z + dd) % 8, (c + cc) % 2), device_id_type=MESH)
    for a, b in poff:
        pl.semaphore_signal(bar, inc=1, device_id=dv(i1 + a, i2 + b), device_id_type=MESH)
    loads = [
        pltpu.make_async_copy(wg_hbm.at[0], wg, wsem.at[0]),
        pltpu.make_async_copy(wu_hbm.at[0], wu, wsem.at[1]),
        pltpu.make_async_copy(wd_hbm.at[0], wd, wsem.at[2]),
    ]
    for cp in loads:
        cp.start()
    stk[0, :, 0:D] = tok_ref[...]
    stk[1, :, 0:D] = og_ref[...]
    lane = lax.broadcasted_iota(jnp.int32, (2, 128), 1)
    dense = jnp.zeros((2, 128), F32)
    for k in range(2):
        dense = dense + jnp.where(lane % 4 == route_ref[:, k : k + 1], gate_ref[:, k : k + 1], 0.0)
    high = dense.astype(BF).astype(F32)
    middle = (dense - high).astype(BF).astype(F32)
    low = dense - high - middle
    codes = jnp.where(lane < 4, high, jnp.where(lane < 8, middle, jnp.where(lane < 12, low, 0.0)))
    stk[0, :, D:W] = codes.astype(BF)
    stk[1, :, D:W] = codes.astype(BF)
    pl.semaphore_wait(bar, 30)

    order = sorted(range(15), key=lambda i: -min(zoff[i][0], 8 - zoff[i][0]))
    me = z * 2 + c
    for i in order:
        dd, cc = zoff[i]
        go(stk.at[(c + cc) % 2], zbuf.at[me], s1.at[i], rv1.at[i], dz((z + dd) % 8, (c + cc) % 2))
    zbuf[me] = stk[c]
    for i in reversed(order):
        dd, cc = zoff[i]
        src = ((z + 8 - dd) % 8) * 2 + (c + cc) % 2
        rc(stk.at[0], zbuf.at[src], s1.at[i], rv1.at[i], dz(0, 0)).wait_recv()
    for i in range(16):
        blk[2 * i : 2 * i + 2, :] = zbuf[i].astype(F32)
    jo = bj(i1, i2)
    mycol = pl.ds(pl.multiple_of(SL * z, 128), SL)
    big[c, jo, :, mycol] = blk[:, mycol].astype(BF)
    big[c, jo, :, CB:W] = blk[:, CB:W].astype(BF)

    for i, (a, b) in enumerate(poff):
        go(big.at[c, jo, :, mycol], big.at[c, jo, :, mycol], sp.at[i], rp.at[i], dv(i1 + a, i2 + b))

    def part(j):
        return big.at[c, j, :, CB:W]

    def opart(j):
        return big.at[c0, j, :, CB:W]

    def a2send(k, a):
        j = bj(i1 + a, i2)
        for t, s in ((0, 1), (1, 3)):
            go(part(j), part(j), sb.at[2 * k + t], rb.at[2 * k + t], dv(i1, i2 + s))

    for a in (1, 3, 2):
        go(part(jo), part(jo), sa.at[a - 1], ra.at[a - 1], dv(i1 + a, i2))
    a2send(0, 0)
    arrivals = {}

    def sibsend(key, ref, oref):
        i = len(arrivals)
        go(ref, ref, ssib.at[i], rsib.at[i], sib)
        arrivals[key] = (oref, i)

    def sibwait(key):
        oref, i = arrivals[key]
        rc(oref, oref, ssib.at[i], rsib.at[i], sib).wait_recv()

    sibsend((0, 0), part(jo), opart(obj(i2, i1)))
    for i, (a, b) in enumerate(poff):
        j = bj(i1 - a + 4, i2 - b + 4)
        rc(big.at[c, jo, :, mycol], big.at[c, j, :, mycol], sp.at[i], rp.at[i], dv(0, 0)).wait_recv()

    def zc(k):
        return pl.ds(pl.multiple_of(SL * ((z + k + 8) % 8), 128), SL)

    def zs_(k):
        return big.at[c, :, :, zc(k)]

    def zh_(k, h):
        return big.at[c, 8 * h : 8 * h + 8, :, zc(k)]

    def zsend(h):
        if h < 3:
            go(zs_(-h), zs_(-h), szp.at[h], rzp.at[h], dz((z + 1) % 8, c))
            go(zs_(h), zs_(h), szm.at[h], rzm.at[h], dz((z + 7) % 8, c))
        else:
            go(zh_(-3, 0), zh_(-3, 0), szp.at[3], rzp.at[3], dz((z + 1) % 8, c))
            go(zh_(3, 1), zh_(3, 1), szm.at[3], rzm.at[3], dz((z + 7) % 8, c))

    def zsib(k):
        sibsend(("z", k), zs_(k), big.at[c0, :, :, zc(k)])

    def zrecv(h):
        if h < 3:
            rc(zs_(0), zs_(-h - 1), szp.at[h], rzp.at[h], dz(0, 0)).wait_recv()
            rc(zs_(0), zs_(h + 1), szm.at[h], rzm.at[h], dz(0, 0)).wait_recv()
            zsib(-h - 1)
            zsib(h + 1)
        else:
            rc(zh_(0, 0), zh_(-4, 0), szp.at[3], rzp.at[3], dz(0, 0)).wait_recv()
            rc(zh_(0, 1), zh_(4, 1), szm.at[3], rzm.at[3], dz(0, 0)).wait_recv()
            zsib(4)

    zsend(0)
    zsib(0)
    for a in (1, 3, 2):
        j = bj(i1 - a + 4, i2)
        rc(part(jo), part(j), sa.at[a - 1], ra.at[a - 1], dv(0, 0)).wait_recv()
        a2send(a, 4 - a)
        sibsend((4 - a, 0), part(j), opart(obj(i2 - a + 4, i1)))

    def half(j, h):
        return big.at[c, j, 16 * h : 16 * h + 16, CB:W]

    def a2recv(k, a):
        jm = bj(i1 + a, i2 + 3)
        jp = bj(i1 + a, i2 + 1)
        rc(part(jo), part(jm), sb.at[2 * k], rb.at[2 * k], dv(0, 0)).wait_recv()
        go(half(jm, 0), half(jm, 0), sf.at[2 * k], rf.at[2 * k], dv(i1, i2 + 1))
        rc(part(jo), part(jp), sb.at[2 * k + 1], rb.at[2 * k + 1], dv(0, 0)).wait_recv()
        go(half(jp, 1), half(jp, 1), sf.at[2 * k + 1], rf.at[2 * k + 1], dv(i1, i2 + 3))
        sibsend((a, 3), part(jm), opart(obj(i2 + a, i1 + 3)))
        sibsend((a, 1), part(jp), opart(obj(i2 + a, i1 + 1)))

    def a2fin(k, a):
        j = bj(i1 + a, i2 + 2)
        rc(half(jo, 0), half(j, 0), sf.at[2 * k], rf.at[2 * k], dv(0, 0)).wait_recv()
        rc(half(jo, 1), half(j, 1), sf.at[2 * k + 1], rf.at[2 * k + 1], dv(0, 0)).wait_recv()
        sibsend((a, 2), part(j), opart(obj(i2 + a, i1 + 2)))

    def rows_of(arr, a):
        if arr == 0:
            return [t * 4 + (y + a) % 4 for t in range(4)]
        return [((x + a) % 4) * 4 + t for t in range(4)]

    def acts_a(offsets):
        for arr in (0, 1):
            js = [j for a in offsets for j in rows_of(arr, a)]
            left = jnp.concatenate([big[arr, j, :, CB:D] for j in js], axis=0)
            if arr == 0:
                made = ((act_g, mm(left, wg[CB:D, :])), (act_u, mm(left, wu[CB:D, :])))
            else:
                made = ((act_h, mmt(left, wd[:, CB:D])),)
            for ref, val in made:
                for i, j in enumerate(js):
                    ref[j] = val[32 * i : 32 * i + 32]

    zrecv(0)
    zsend(1)
    a2recv(0, 0)
    zrecv(1)
    zsend(2)
    a2recv(1, 3)
    a2recv(3, 1)
    zrecv(2)
    zsend(3)
    a2fin(0, 0)
    a2recv(2, 2)
    a2fin(1, 3)
    for cp in loads:
        cp.wait()
    for a in (0, 3):
        for b in range(4):
            sibwait((a, b))
    acts_a((0, 3))
    a2fin(3, 1)
    zrecv(3)
    a2fin(2, 2)
    for a in (1, 2):
        for b in range(4):
            sibwait((a, b))
    acts_a((1, 2))
    for k in range(-3, 5):
        sibwait(("z", k))
    save = [pltpu.make_async_copy(big, bigo, osem.at[0])]
    save[0].start()

    lane32 = lax.broadcasted_iota(jnp.int32, (128, 128), 1)
    own_lane = (lane32 % 4 == e) & (lane32 < 12)

    def hidden_rows(r, _):
        def get(arr, lo, hi):
            return big[arr, pl.ds(4 * r, 4), :, lo:hi].reshape(128, hi - lo)

        rows_x = get(0, 0, CB)
        g = act_g[pl.ds(4 * r, 4)].reshape(128, FB) + mm(rows_x, wg[0:CB, :])
        u = act_u[pl.ds(4 * r, 4)].reshape(128, FB) + mm(rows_x, wu[0:CB, :])
        h = act_h[pl.ds(4 * r, 4)].reshape(128, FB) + mmt(get(1, 0, CB), wd[:, 0:CB])
        gate = jnp.sum(jnp.where(own_lane, get(1, D, W).astype(F32), 0.0), axis=1, keepdims=True)
        sig = jax.nn.sigmoid(g)
        silu = g * sig
        h = h * gate
        hs[pl.ds(4 * r, 4)] = (gate * (silu * u)).astype(BF).reshape(4, 32, FB)
        gu[pl.ds(4 * r, 4), :, 0:FB] = (h * u * sig * (1.0 + g * (1.0 - sig))).astype(BF).reshape(4, 32, FB)
        gu[pl.ds(4 * r, 4), :, FB : 2 * FB] = (h * silu).astype(BF).reshape(4, 32, FB)
        return 0

    lax.fori_loop(0, 4, hidden_rows, 0)
    save += [
        pltpu.make_async_copy(gu, guo, osem.at[1]),
        pltpu.make_async_copy(hs, hso, osem.at[2]),
    ]
    save[1].start()
    save[2].start()

    js = [bj(i1 + a, i2 + b) for b in range(4) for a in range(4)]

    def share(q, half_of):
        cols = pl.ds(pl.multiple_of(half_of * HW + q * QC, QC), QC)
        left = jnp.concatenate([gu[j] for j in js], axis=0)
        return mmt(left[:, 0:FB], wg[cols, :]) + mmt(left[:, FB : 2 * FB], wu[cols, :])

    for q in range(NQ):
        pgo[q] = share(q, c0).astype(BF).reshape(16, 32, QC)
        go(pgo.at[q], sbuf.at[q], ss0.at[q], rs0.at[q], sib)
    for q in range(NQ):
        val = share(q, c).reshape(16, 32, QC)
        rc(pgo.at[q], sbuf.at[q], ss0.at[q], rs0.at[q], sib).wait_recv()
        for b in (2, 1, 3, 0):
            for a in range(4):
                s = val[b * 4 + a] + sbuf[q, a * 4 + b].astype(F32)
                if b:
                    acc[q, b - 1, a] = s.astype(BF)
                else:
                    own1[q, a] = s
            if b:
                i = q * 3 + b - 1
                go(acc.at[q, b - 1], r1.at[q, b - 1], ss1.at[i], rs1.at[i], dv(i1, i2 + b))
    for q in range(NQ):
        for b in (1, 3, 2):
            i = q * 3 + b - 1
            rc(acc.at[q, b - 1], r1.at[q, b - 1], ss1.at[i], rs1.at[i], dv(0, 0)).wait_recv()
        for a in (2, 1, 3, 0):
            s = own1[q, a] + r1[q, 0, a].astype(F32) + r1[q, 1, a].astype(F32) + r1[q, 2, a].astype(F32)
            if a:
                i = q * 3 + a - 1
                acc1[q, a - 1] = s.astype(BF)
                go(acc1.at[q, a - 1], r2.at[q, a - 1], ss2.at[i], rs2.at[i], dv(i1 + a, i2))
            else:
                own2[q] = s
    for q in range(NQ):
        for a in (1, 3, 2):
            i = q * 3 + a - 1
            rc(acc1.at[q, a - 1], r2.at[q, a - 1], ss2.at[i], rs2.at[i], dv(0, 0)).wait_recv()
        own2[q] = own2[q] + r2[q, 0].astype(F32) + r2[q, 1].astype(F32) + r2[q, 2].astype(F32)
        for i in range(16):
            zs[i, :, q * QC : q * QC + QC] = own2[q, 2 * i : 2 * i + 2, :].astype(BF)
    for i in order:
        dd, cc = zoff[i]
        to = ((z + dd) % 8) * 2 + (c + cc) % 2
        go(zs.at[to], r3.at[z, c], ss3.at[i], rs3.at[i], dz((z + dd) % 8, (c + cc) % 2))
    r3[z, c] = zs[me]
    for i in reversed(order):
        dd, cc = zoff[i]
        rc(zs.at[0], r3.at[(z + 8 - dd) % 8, (c + cc) % 2], ss3.at[i], rs3.at[i], dz(0, 0)).wait_recv()
    for h in range(2):
        s = r3[0, h].astype(F32)
        for k in range(1, 8):
            s = s + r3[k, h].astype(F32)
        out[:, h * HW : (h + 1) * HW] = s.astype(BF)
    for cp in sends:
        cp.wait_send()
    for cp in save:
        cp.wait()


def main_call(*args):
    dma = pltpu.SemaphoreType.DMA
    V = pltpu.VMEM
    vm = pl.BlockSpec(memory_space=V)
    hbm = pl.BlockSpec(memory_space=pl.ANY)
    return pl.pallas_call(
        main_kernel,
        out_shape=(
            jax.ShapeDtypeStruct((2, D), BF),
            jax.ShapeDtypeStruct((2, 16, 32, W), BF),
            jax.ShapeDtypeStruct((16, 32, 2 * FB), BF),
            jax.ShapeDtypeStruct((16, 32, FB), BF),
        ),
        in_specs=[vm, vm, vm, vm, hbm, hbm, hbm],
        out_specs=(vm, hbm, hbm, hbm),
        scratch_shapes=[
            V((2, 16, 32, W), BF), V((2, 2, W), BF), V((16, 2, W), BF), V((32, W), F32),
            V((D, FB), BF), V((D, FB), BF), V((FB, D), BF),
            V((16, 32, FB), F32), V((16, 32, FB), F32), V((16, 32, FB), F32),
            V((16, 32, 2 * FB), BF), V((16, 32, FB), BF),
            V((NQ, 16, 32, QC), BF), V((NQ, 16, 32, QC), BF), V((NQ, 3, 4, 32, QC), BF), V((NQ, 4, 32, QC), F32),
            V((NQ, 3, 4, 32, QC), BF), V((NQ, 3, 32, QC), BF), V((NQ, 3, 32, QC), BF), V((NQ, 32, QC), F32),
            V((16, 2, HW), BF), V((8, 2, 2, HW), BF),
            dma((3,)), dma((3,)), dma((15,)), dma((15,)), dma((15,)), dma((15,)), dma((3,)), dma((3,)),
            dma((8,)), dma((8,)), dma((8,)), dma((8,)), dma((4,)), dma((4,)), dma((4,)), dma((4,)),
            dma((24,)), dma((24,)), dma((NQ,)), dma((NQ,)), dma((3 * NQ,)), dma((3 * NQ,)),
            dma((3 * NQ,)), dma((3 * NQ,)), dma((15,)), dma((15,)),
        ],
        compiler_params=pltpu.CompilerParams(
            collective_id=0, has_side_effects=True, vmem_limit_bytes=60 << 20
        ),
        name="gather_compute_sum",
    )(*args)


def contract_rows(left, right):
    return lax.dot_general(left, right, (((0,), (0,)), ((), ())), preferred_element_type=F32)


def per_device(tokens, routes, gates, out_grad, gate_weight, up_weight, down_weight):
    tokens_grad, big, gu, hs = main_call(tokens, routes, gates, out_grad, gate_weight, up_weight, down_weight)
    big = big.reshape(2, 512, W)
    gu = gu.reshape(512, 2 * FB)
    return (
        tokens_grad,
        contract_rows(big[0, :, :D], gu[:, :FB]).astype(BF)[None],
        contract_rows(big[0, :, :D], gu[:, FB:]).astype(BF)[None],
        contract_rows(hs.reshape(512, FB), big[1, :, :D]).astype(BF)[None],
    )


def solution(mesh):
    return jax.shard_map(
        per_device,
        mesh=mesh,
        in_specs=(
            P(("expert", "fsdp"), None),
            P(("expert", "fsdp"), None),
            P(("expert", "fsdp"), None),
            P(("expert", "fsdp"), None),
            P("expert", None, "fsdp"),
            P("expert", None, "fsdp"),
            P("expert", "fsdp", None),
        ),
        out_specs=(
            P(("expert", "fsdp"), None),
            P("expert", None, "fsdp"),
            P("expert", None, "fsdp"),
            P("expert", "fsdp", None),
        ),
        check_vma=False,
    )
```

time: 668 us -> 93 us (0.14)
  waiting for transfers between devices: 367 us -> 0 us
  blocking collectives: 193 us -> 0 us
  Pallas kernels: 0 us -> 80.9 us
  starting transfers between devices: 53.4 us -> 0 us
  matrix products: 30.2 us -> 10.2 us
  between operations: 14.5 us -> 0.66 us
    reduce_scatter x1 -> x0, waiting for transfers between devices: 366 us -> none  [per_device(): lax.psum_scatter(contract(gate_rows, w_gate, 1, 1) + contract(up_rows, w_...]
    unnamed x1 -> x0, blocking collectives: 178 us -> none
    pallas_call x0 -> x1, Pallas kernels: none -> 80.9 us  [main_call(): pl.pallas_call(main_kernel, out_shape=(jax.ShapeDtypeStruct((2, D), BF),...]
    all_to_all x2 -> x0, starting transfers between devices: 53.3 us -> none  [the longest x1 49.2 us: per_device(): lax.all_to_all(row_grad, 'expert', split_axis=0, concat_axis=0, tiled=True)]
    dot_general x11 -> x3, matrix products: 30.2 us -> 10.2 us  [contract_rows(): lax.dot_general(left, right, (((0,), (0,)), ((), ())), preferred_element_...]
    all_to_all x2 -> x0, blocking collectives: 15.3 us -> none  [the longest x1 8.86 us: per_device(): lax.all_to_all(send_x, 'expert', split_axis=0, concat_axis=0, tiled=True)]
  transfers between devices with their start and end apart: 5 -> 0, of which waited for: 2 -> 0; matrix products, arithmetic and copies ran while one was open for 3% -> 0% of each run, Pallas kernels for 0% -> 0%
where the time goes in v2:
time: 93 us; the launch traced here: 92.9 us
  Pallas kernels  80.9 us (87%)
  matrix products  10.2 us (11%)
  local copies, waits for them, and re-layouts  1.03 us (1%)
    pallas_call x1, Pallas kernels, main_call(): pl.pallas_call(main_kernel, out_shape=(jax.ShapeDtypeStruct((2, D), BF),...  80.9 us
    dot_general x3, matrix products, contract_rows(): lax.dot_general(left, right, (((0,), (0,)), ((), ())), preferred_element_...  10.2 us

profile of v2, /device:TPU:1, one launch (start us, length us, event | category | flops | bytes accessed | tf_op | source)
XLA Modules:
  0.0 92.9 jit_solution(793066614039202416)
XLA Ops:
  0.6 80.9 %gather_compute_sum.1 = (bf16[2,4096]{1,0:T(2,128)(2,1)}, bf16[2,16,32,4224]{3,2,1,0:T(8,128)(2,1)}, bf16[16,32,512]{2,1,0:T(8,128)(2,1)}, bf16[16,32,256]{2,1,0:T(8,128)(2,1)}) custom-call(bf16[2,4096]{1,0:T(2,128)(2,1)} %tok_ref.1, s32[2,2]{1,0:T(2,128)} %route_ref.1, f32[2,2]{1,0:T(2,128)} %gate_ref.1, bf16[2,4096]{1,0:T(2,128)(2,1)} %og_ref.1, ...), custom_call_target="tpu_custom_call" | custom-call | tf_op jit(solution)/shard_map/gather_compute_sum/pallas_call | solution.py:354
  81.6 0.0 copy-start
  81.6 0.0 copy-start.3
  81.6 5.0 %fusion = bf16[1,4096,256]{2,1,0:T(8,128)(2,1)} fusion(bf16[2,512,4224]{2,1,0:T(8,128)(2,1)} %bitcast.17, bf16[512,512]{1,0:T(8,128)(2,1)} %bitcast.21), kind=kOutput, calls=%fused_computation.3 | convolution fusion | flops 1074790400 | bytes 6553600 | tf_op jit(solution)/shard_map/dot_general | solution.py:385
  86.6 0.0 copy-done
  86.6 0.4 copy-done.3
  87.0 0.0 copy-start.1
  87.0 2.6 %fusion.1 = bf16[1,4096,256]{2,1,0:T(8,128)(2,1)} fusion(bf16[2,512,4224]{2,1,0:T(8,128)(2,1)S(1)} %bitcast.18, bf16[512,512]{1,0:T(8,128)(2,1)S(1)} %bitcast.22), kind=kOutput, calls=%fused_computation.4 | convolution fusion | flops 1074790400 | bytes 6553600 | tf_op jit(solution)/shard_map/dot_general | solution.py:385
  89.6 0.0 copy-start.2
  89.6 0.0 copy-done.1
  89.6 2.6 %fusion.2 = bf16[1,256,4096]{2,1,0:T(8,128)(2,1)} fusion(bf16[512,256]{1,0:T(8,128)(2,1)S(1)} %bitcast.20, bf16[2,512,4224]{2,1,0:T(8,128)(2,1)S(1)} %bitcast.19), kind=kOutput, calls=%fused_computation.5 | convolution fusion | flops 1074790400 | bytes 6553600 | tf_op jit(solution)/shard_map/dot_general | solution.py:385
  92.3 0.0 copy-done.2
  92.3 0.6 copy.12
Async XLA Ops:
  81.6 5.0 %copy-start = (bf16[2,16,32,4224]{3,2,1,0:T(8,128)(2,1)S(1)}, bf16[2,16,32,4224]{3,2,1,0:T(8,128)(2,1)}, u32[]{:S(2)}) copy-start(bf16[2,16,32,4224]{3,2,1,0:T(8,128)(2,1)} %get-tuple-element.9) | copy-start | bytes 25952260
  81.6 5.4 %copy-start.3 = (bf16[16,32,512]{2,1,0:T(8,128)(2,1)S(1)}, bf16[16,32,512]{2,1,0:T(8,128)(2,1)}, u32[]{:S(2)}) copy-start(bf16[16,32,512]{2,1,0:T(8,128)(2,1)} %get-tuple-element.10) | copy-start | bytes 1572868
  87.0 2.6 %copy-start.1 = (bf16[16,32,256]{2,1,0:T(8,128)(2,1)S(1)}, bf16[16,32,256]{2,1,0:T(8,128)(2,1)}, u32[]{:S(2)}) copy-start(bf16[16,32,256]{2,1,0:T(8,128)(2,1)} %get-tuple-element.11) | copy-start | bytes 786436
  89.6 2.6 %copy-start.2 = (bf16[2,4096]{1,0:T(2,128)(2,1)S(1)}, bf16[2,4096]{1,0:T(2,128)(2,1)}, u32[]{:S(2)}) copy-start(bf16[2,4096]{1,0:T(2,128)(2,1)} %get-tuple-element.16) | copy-start | bytes 49156

commit v3 on v2

v3 whole, which is shorter than its diff:
```python
import jax
import jax.numpy as jnp
from jax import lax
from jax.experimental import pallas as pl
from jax.experimental.pallas import tpu as pltpu
from jax.sharding import PartitionSpec as P

MESH = pl.DeviceIdType.MESH
BF = jnp.bfloat16
F32 = jnp.float32
D = 4096
FB = 256
SL = 128
CB = 8 * SL
W = D + 128
CM = (CB + D) // 2
SEG = ((CB, CM), (CM, W))
DATA = ((CB, CM), (CM, D))
SUB = 4
HW = D // 2
QC = 512
NQ = HW // QC


def mm(left, right):
    return lax.dot_general(left, right, (((1,), (0,)), ((), ())), preferred_element_type=F32)


def mmt(left, right):
    return lax.dot_general(left, right, (((1,), (1,)), ((), ())), preferred_element_type=F32)


def main_kernel(
    tok_ref, route_ref, gate_ref, og_ref, wg_hbm, wu_hbm, wd_hbm,
    out, dwg_hbm, dwu_hbm, dwd_hbm,
    big, stk, zbuf, blk, wg, wu, wd, act, gu, hs, hst, dwg, dwu, dwd,
    pgo, sbuf, far, far_in, near, kept, joined, own1, r1, acc1, r2, own2, zs, r3,
    wsem, osem, s1, rv1, sp, rp, sa, ra, sb, rb, sf, rf, szp, rzp, szm, rzm, ssib, rsib,
    ss0, rs0, ss1, rs1, ss2, rs2, ss3, rs3,
):
    e = lax.axis_index("expert")
    f = lax.axis_index("fsdp")
    c = lax.rem(e, 2)
    zl = lax.div(e, 2)
    xy = lax.div(f, 4)
    zh = lax.rem(f, 4)
    z = zh * 2 + zl
    x = lax.div(f, 16)
    y = lax.rem(xy, 4)
    c0 = 1 - c
    i1 = y * c0 + x * c
    i2 = x * c0 + y * c
    w1 = [lax.rem(i1 + a, 4) * (c0 + 4 * c) for a in range(4)]
    w2 = [lax.rem(i2 + a, 4) * (4 * c0 + c) for a in range(4)]
    zz = [lax.rem(z + d, 8) for d in range(8)]
    zdev = [(lax.rem(v, 2) * 2, xy * 4 + lax.div(v, 2)) for v in zz]
    core = [c, c0]

    def bj(a, b):
        return w1[a % 4] + w2[b % 4]

    def dv(a, b):
        return {"expert": e, "fsdp": bj(a, b) * 4 + zh}

    def dz(d, cc):
        return {"expert": zdev[d % 8][0] + core[cc], "fsdp": zdev[d % 8][1]}

    sib = {"expert": zl * 2 + c0, "fsdp": f}

    def rc(src, dst, ss, rs, d):
        return pltpu.make_async_remote_copy(
            src_ref=src, dst_ref=dst, send_sem=ss, recv_sem=rs, device_id=d, device_id_type=MESH
        )

    sends = []

    def go(*args):
        cp = rc(*args)
        cp.start()
        sends.append(cp)

    bar = pltpu.get_barrier_semaphore()
    zoff = [(dd, cc) for dd in range(8) for cc in range(2) if (dd, cc) != (0, 0)]
    poff = [(a, b) for a in range(4) for b in range(4) if (a, b) != (0, 0)]
    for dd, cc in zoff:
        pl.semaphore_signal(bar, inc=1, device_id=dz(dd, cc), device_id_type=MESH)
    for a, b in poff:
        pl.semaphore_signal(bar, inc=1, device_id=dv(a, b), device_id_type=MESH)
    loads = [
        pltpu.make_async_copy(wg_hbm.at[0], wg, wsem.at[0]),
        pltpu.make_async_copy(wu_hbm.at[0], wu, wsem.at[1]),
        pltpu.make_async_copy(wd_hbm.at[0], wd, wsem.at[2]),
    ]
    for cp in loads:
        cp.start()
    stk[0, :, 0:D] = tok_ref[...]
    stk[1, :, 0:D] = og_ref[...]
    lane = lax.broadcasted_iota(jnp.int32, (2, 128), 1)
    dense = jnp.zeros((2, 128), F32)
    for k in range(2):
        dense = dense + jnp.where(lane % 4 == route_ref[:, k : k + 1], gate_ref[:, k : k + 1], 0.0)
    high = dense.astype(BF).astype(F32)
    middle = (dense - high).astype(BF).astype(F32)
    low = dense - high - middle
    codes = jnp.where(lane < 4, high, jnp.where(lane < 8, middle, jnp.where(lane < 12, low, 0.0)))
    stk[0, :, D:W] = codes.astype(BF)
    stk[1, :, D:W] = codes.astype(BF)
    pl.semaphore_wait(bar, 30)

    order = sorted(range(15), key=lambda i: -min(zoff[i][0], 8 - zoff[i][0]))
    me = z * 2 + c
    line = ((0, CM), (CM, W))
    for t, (lo, hi) in enumerate(line):
        for i in order:
            dd, cc = zoff[i]
            go(
                stk.at[core[cc], :, lo:hi], zbuf.at[me, :, lo:hi], s1.at[15 * t + i], rv1.at[15 * t + i], dz(dd, cc)
            )
    zbuf[me] = stk[c]
    jo = bj(0, 0)
    mycol = pl.ds(pl.multiple_of(SL * z, 128), SL)

    def take_line(t):
        lo, hi = line[t]
        for i in reversed(order):
            dd, cc = zoff[i]
            src = zz[(8 - dd) % 8] * 2 + core[cc]
            rc(stk.at[0, :, lo:hi], zbuf.at[src, :, lo:hi], s1.at[15 * t + i], rv1.at[15 * t + i], sib).wait_recv()
        for i in range(16):
            blk[2 * i : 2 * i + 2, lo:hi] = zbuf[i, :, lo:hi].astype(F32)
        if t == 0:
            big[c, jo, :, mycol] = blk[:, mycol].astype(BF)
        lo, hi = SEG[t]
        big[c, jo, :, lo:hi] = blk[:, lo:hi].astype(BF)

    def gj(g, a, b):
        return bj(a, b) if g == 0 else bj(b, a)

    def gdv(g, a, b):
        return dv(a, b) if g == 0 else dv(b, a)

    def part(g, j):
        return big.at[c, j, :, SEG[g][0] : SEG[g][1]]

    def a2send(g, k, a):
        j = gj(g, a, 0)
        for t, s in ((0, 1), (1, 3)):
            i = 8 * g + 2 * k + t
            go(part(g, j), part(g, j), sb.at[i], rb.at[i], gdv(g, 0, s))

    arrivals = {}

    def sibsend(key, ref, oref=None):
        i = len(arrivals)
        go(ref, ref, ssib.at[i], rsib.at[i], sib)
        if oref is None:
            g, a, b = key
            oref = big.at[c0, gj(g, b, a), :, SEG[g][0] : SEG[g][1]]
        arrivals[key] = (oref, i)

    def sibwait(key):
        oref, i = arrivals[key]
        rc(oref, oref, ssib.at[i], rsib.at[i], sib).wait_recv()

    def own_send(g):
        for a in (1, 3, 2):
            i = 3 * g + a - 1
            go(part(g, jo), part(g, jo), sa.at[i], ra.at[i], gdv(g, a, 0))
        a2send(g, 0, 0)
        sibsend((g, 0, 0), part(g, jo))

    def a1recv(g):
        for a in (1, 3, 2):
            j = gj(g, 4 - a, 0)
            i = 3 * g + a - 1
            rc(part(g, jo), part(g, j), sa.at[i], ra.at[i], sib).wait_recv()
            a2send(g, a, 4 - a)
            sibsend((g, 4 - a, 0), part(g, j))

    def half(g, j, h):
        return big.at[c, j, 16 * h : 16 * h + 16, SEG[g][0] : SEG[g][1]]

    slot = {0: 0, 3: 1, 2: 2, 1: 3}

    def a2recv(g, a):
        for h, b in ((0, 3), (1, 1)):
            j = gj(g, a, b)
            i = 8 * g + 2 * slot[a] + h
            rc(part(g, jo), part(g, j), sb.at[i], rb.at[i], sib).wait_recv()
            go(half(g, j, h), half(g, j, h), sf.at[i], rf.at[i], gdv(g, 0, 4 - b))
        for b in (3, 1):
            sibsend((g, a, b), part(g, gj(g, a, b)))

    def a2fin(g, a):
        j = gj(g, a, 2)
        for h in range(2):
            i = 8 * g + 2 * slot[a] + h
            rc(half(g, jo, h), half(g, j, h), sf.at[i], rf.at[i], sib).wait_recv()
        sibsend((g, a, 2), part(g, j))

    def zc(k):
        return pl.ds(pl.multiple_of(SL * zz[k % 8], 128), SL)

    def piece(k, u):
        n = 16 // SUB
        return big.at[c, n * u : n * u + n, :, zc(k)]

    def zsend(h, u):
        i = SUB * h + u
        if h < 3 or u < SUB // 2:
            go(piece(-h, u), piece(-h, u), szp.at[i], rzp.at[i], dz(1, 0))
        if h < 3 or u >= SUB // 2:
            go(piece(h, u), piece(h, u), szm.at[i], rzm.at[i], dz(7, 0))

    def zsib(k):
        sibsend(("z", k), big.at[c, :, :, zc(k)], big.at[c0, :, :, zc(k)])

    def zrecv(h):
        for u in range(SUB):
            i = SUB * h + u
            if h < 3 or u < SUB // 2:
                rc(piece(0, u), piece(-h - 1, u), szp.at[i], rzp.at[i], sib).wait_recv()
            if h < 3 or u >= SUB // 2:
                rc(piece(0, u), piece(h + 1, u), szm.at[i], rzm.at[i], sib).wait_recv()
            if h < 3:
                zsend(h + 1, u)
        zsib(-h - 1)
        if h < 3:
            zsib(h + 1)

    take_line(0)
    for i, (a, b) in enumerate(poff):
        go(big.at[c, jo, :, mycol], big.at[c, jo, :, mycol], sp.at[i], rp.at[i], dv(a, b))
    own_send(0)
    take_line(1)
    own_send(1)
    for i, (a, b) in enumerate(poff):
        rc(big.at[c, jo, :, mycol], big.at[c, bj(4 - a, 4 - b), :, mycol], sp.at[i], rp.at[i], sib).wait_recv()
    for u in range(SUB):
        zsend(0, u)
    zsib(0)

    def rows_of(arr, a):
        if arr == 0:
            return [t * 4 + lax.rem(y + a, 4) for t in range(4)]
        return [lax.rem(x + a, 4) * 4 + t for t in range(4)]

    def acts(t, arr, js, lo, hi):
        left = jnp.concatenate([big[arr, j, :, lo:hi] for j in js], axis=0)
        if arr == 0:
            made = ((0, mm(left, wg[lo:hi, :])), (1, mm(left, wu[lo:hi, :])))
        else:
            made = ((2, mmt(left, wd[:, lo:hi])),)
        for n, val in made:
            for i, j in enumerate(js):
                act[t, n, j] = val[32 * i : 32 * i + 32]

    def acts_a(g, offsets):
        for a in offsets:
            for b in range(4):
                sibwait((g, a, b))
        for arr in (0, 1):
            acts(g, arr, [j for a in offsets for j in rows_of(arr ^ g, a)], *DATA[g])

    a1recv(0)
    a2recv(0, 0)
    zrecv(0)
    a1recv(1)
    a2recv(0, 3)
    zrecv(1)
    a2recv(1, 0)
    a2recv(0, 1)
    a2fin(0, 0)
    zrecv(2)
    a2recv(0, 2)
    a2recv(1, 3)
    a2recv(1, 1)
    a2fin(0, 3)
    a2fin(0, 1)
    a2fin(1, 0)
    a2recv(1, 2)
    for cp in loads:
        cp.wait()
    acts_a(0, (0, 3))
    zrecv(3)
    a2fin(0, 2)
    a2fin(1, 3)
    a2fin(1, 1)
    acts_a(0, (1, 2))
    a2fin(1, 2)
    acts_a(1, (0, 3))
    for k in range(-4, 4):
        sibwait(("z", k))
    for arr in (0, 1):
        acts(2, arr, list(range(16)), 0, CB)
    acts_a(1, (1, 2))

    lane32 = lax.broadcasted_iota(jnp.int32, (128, 128), 1)
    own_lane = (lane32 % 4 == e) & (lane32 < 12)

    def hidden_rows(r, _):
        def get(arr, lo, hi):
            return big[arr, pl.ds(4 * r, 4), :, lo:hi].reshape(128, hi - lo)

        def added(n):
            return sum(act[t, n, pl.ds(4 * r, 4)].reshape(128, FB) for t in range(3))

        g = added(0)
        u = added(1)
        h = added(2)
        gate = jnp.sum(jnp.where(own_lane, get(1, D, W).astype(F32), 0.0), axis=1, keepdims=True)
        sig = jax.nn.sigmoid(g)
        silu = g * sig
        h = h * gate
        hs[pl.ds(4 * r, 4)] = (gate * (silu * u)).astype(BF).reshape(4, 32, FB)
        gu[pl.ds(4 * r, 4), :, 0:FB] = (h * u * sig * (1.0 + g * (1.0 - sig))).astype(BF).reshape(4, 32, FB)
        gu[pl.ds(4 * r, 4), :, FB : 2 * FB] = (h * silu).astype(BF).reshape(4, 32, FB)
        return 0

    lax.fori_loop(0, 4, hidden_rows, 0)
    save = []

    def store(refs):
        for a, b in refs:
            cp = pltpu.make_async_copy(a, b, osem.at[len(save)])
            cp.start()
            save.append(cp)

    def weight_grads(t):
        cols = slice(512 * t, 512 * t + 512)
        val = lax.dot_general(
            big[0, :, :, cols].reshape(512, 512),
            gu[...].reshape(512, 2 * FB),
            (((0,), (0,)), ((), ())),
            preferred_element_type=F32,
        ).astype(BF)
        dwg[cols, :] = val[:, 0:FB]
        dwu[cols, :] = val[:, FB : 2 * FB]
        dwd[:, cols] = mm(hst[...], big[1, :, :, cols].reshape(512, 512)).astype(BF)
        store(
            [
                (dwg.at[cols, :], dwg_hbm.at[0, cols, :]),
                (dwu.at[cols, :], dwu_hbm.at[0, cols, :]),
                (dwd.at[:, cols], dwd_hbm.at[0, :, cols]),
            ]
        )

    def sj(q, a, b):
        return bj(a, b) if q % 2 == 0 else bj(b, a)

    def sdv(q, a, b):
        return dv(a, b) if q % 2 == 0 else dv(b, a)

    def share(q, half_of):
        cols = pl.ds(pl.multiple_of(half_of * HW + q * QC, QC), QC)
        left = jnp.concatenate([gu[sj(q, a, b)] for b in range(4) for a in range(4)], axis=0)
        return mmt(left[:, 0:FB], wg[cols, :]) + mmt(left[:, FB : 2 * FB], wu[cols, :])

    def sum_send(q):
        val = share(q, c).reshape(16, 32, QC)
        rc(pgo.at[q], sbuf.at[q], ss0.at[q], rs0.at[q], sib).wait_recv()

        def at(a, b):
            return val[b * 4 + a] + sbuf[q, a * 4 + b].astype(F32)

        for a in range(4):
            far[q, a] = at(a, 2).astype(BF)
        for h, b in ((0, 1), (1, 3)):
            i = 6 * q + h
            go(far.at[q, 2 * h : 2 * h + 2], far_in.at[q, h], ss1.at[i], rs1.at[i], sdv(q, 0, b))
        for h, b in ((0, 1), (1, 3)):
            i = 6 * q + 2 + h
            for a in range(2):
                near[q, h, a] = at(2 - 2 * h + a, b).astype(BF)
                kept[q, h, a] = at(2 * h + a, b)
            go(near.at[q, h], r1.at[q, h, 2 - 2 * h : 4 - 2 * h], ss1.at[i], rs1.at[i], sdv(q, 0, b))
        for a in range(4):
            own1[q, a] = at(a, 0)

    def join(q):
        for h, b in ((0, 1), (1, 3)):
            i = 6 * q + h
            rc(far.at[q, 0:2], far_in.at[q, h], ss1.at[i], rs1.at[i], sib).wait_recv()
            joined[q, h] = (kept[q, h] + far_in[q, h].astype(F32)).astype(BF)
            i = 6 * q + 4 + h
            go(joined.at[q, h], r1.at[q, h, 2 * h : 2 * h + 2], ss1.at[i], rs1.at[i], sdv(q, 0, b))

    def second(q):
        for h in range(2):
            for i, lo in ((6 * q + 2 + h, 2 - 2 * h), (6 * q + 4 + h, 2 * h)):
                rc(near.at[q, h], r1.at[q, h, lo : lo + 2], ss1.at[i], rs1.at[i], sib).wait_recv()
        for a in (2, 1, 3, 0):
            s = own1[q, a] + r1[q, 0, a].astype(F32) + r1[q, 1, a].astype(F32)
            if a:
                i = q * 3 + a - 1
                acc1[q, a - 1] = s.astype(BF)
                go(acc1.at[q, a - 1], r2.at[q, a - 1], ss2.at[i], rs2.at[i], sdv(q, a, 0))
            else:
                own2[q] = s

    def third(q):
        for a in (1, 3, 2):
            i = q * 3 + a - 1
            rc(acc1.at[q, a - 1], r2.at[q, a - 1], ss2.at[i], rs2.at[i], sib).wait_recv()
        own2[q] = own2[q] + r2[q, 0].astype(F32) + r2[q, 1].astype(F32) + r2[q, 2].astype(F32)
        for i in range(16):
            zs[q // 2, i, :, q % 2 * QC : q % 2 * QC + QC] = own2[q, 2 * i : 2 * i + 2, :].astype(BF)

    def line_send(t):
        for i in order:
            dd, cc = zoff[i]
            go(zs.at[t, zz[dd] * 2 + core[cc]], r3.at[t, z, c], ss3.at[15 * t + i], rs3.at[15 * t + i], dz(dd, cc))
        r3[t, z, c] = zs[t, me]

    def line_sum(t):
        for i in reversed(order):
            dd, cc = zoff[i]
            here = r3.at[t, zz[(8 - dd) % 8], core[cc]]
            rc(zs.at[t, 0], here, ss3.at[15 * t + i], rs3.at[15 * t + i], sib).wait_recv()
        for h in range(2):
            s = r3[t, 0, h].astype(F32)
            for k in range(1, 8):
                s = s + r3[t, k, h].astype(F32)
            out[:, h * HW + t * HW // 2 : h * HW + (t + 1) * HW // 2] = s.astype(BF)

    for q in range(NQ):
        pgo[q] = share(q, c0).astype(BF).reshape(16, 32, QC)
        go(pgo.at[q], sbuf.at[q], ss0.at[q], rs0.at[q], sib)
    for q in range(NQ):
        sum_send(q)
        if q:
            join(q - 1)
    hst[...] = hs[...].reshape(512, FB).astype(F32).T.astype(BF)
    join(NQ - 1)
    weight_grads(0)
    second(0)
    weight_grads(1)
    second(1)
    weight_grads(2)
    second(2)
    weight_grads(3)
    second(3)
    third(0)
    third(1)
    line_send(0)
    weight_grads(4)
    third(2)
    third(3)
    line_send(1)
    weight_grads(5)
    weight_grads(6)
    weight_grads(7)
    line_sum(0)
    line_sum(1)
    for cp in sends:
        cp.wait_send()
    for cp in save:
        cp.wait()


def main_call(*args):
    dma = pltpu.SemaphoreType.DMA
    V = pltpu.VMEM
    vm = pl.BlockSpec(memory_space=V)
    hbm = pl.BlockSpec(memory_space=pl.ANY)
    return pl.pallas_call(
        main_kernel,
        out_shape=(
            jax.ShapeDtypeStruct((2, D), BF),
            jax.ShapeDtypeStruct((1, D, FB), BF),
            jax.ShapeDtypeStruct((1, D, FB), BF),
            jax.ShapeDtypeStruct((1, FB, D), BF),
        ),
        in_specs=[vm, vm, vm, vm, hbm, hbm, hbm],
        out_specs=(vm, hbm, hbm, hbm),
        scratch_shapes=[
            V((2, 16, 32, W), BF), V((2, 2, W), BF), V((16, 2, W), BF), V((32, W), F32),
            V((D, FB), BF), V((D, FB), BF), V((FB, D), BF),
            V((3, 3, 16, 32, FB), F32),
            V((16, 32, 2 * FB), BF), V((16, 32, FB), BF), V((FB, 512), BF),
            V((D, FB), BF), V((D, FB), BF), V((FB, D), BF),
            V((NQ, 16, 32, QC), BF), V((NQ, 16, 32, QC), BF), V((NQ, 4, 32, QC), BF), V((NQ, 2, 2, 32, QC), BF),
            V((NQ, 2, 2, 32, QC), BF), V((NQ, 2, 2, 32, QC), F32), V((NQ, 2, 2, 32, QC), BF), V((NQ, 4, 32, QC), F32),
            V((NQ, 2, 4, 32, QC), BF), V((NQ, 3, 32, QC), BF), V((NQ, 3, 32, QC), BF), V((NQ, 32, QC), F32),
            V((2, 16, 2, HW // 2), BF), V((2, 8, 2, 2, HW // 2), BF),
            dma((3,)), dma((24,)), dma((30,)), dma((30,)), dma((15,)), dma((15,)), dma((6,)), dma((6,)),
            dma((16,)), dma((16,)), dma((16,)), dma((16,)), dma((4 * SUB,)), dma((4 * SUB,)), dma((4 * SUB,)), dma((4 * SUB,)),
            dma((40,)), dma((40,)), dma((NQ,)), dma((NQ,)), dma((6 * NQ,)), dma((6 * NQ,)),
            dma((3 * NQ,)), dma((3 * NQ,)), dma((30,)), dma((30,)),
        ],
        compiler_params=pltpu.CompilerParams(
            collective_id=0, has_side_effects=True, vmem_limit_bytes=60 << 20
        ),
        name="gather_compute_sum",
    )(*args)


def copy_kernel(*refs):
    loads, stores = [], []
    for a, b, held in zip(refs[0:4], refs[4:8], refs[8:12]):
        pieces = 4 if a.shape[0] == 1 else 1
        n = a.shape[1] // pieces
        for i in range(pieces):
            at = (slice(None), slice(n * i, n * i + n)) if pieces > 1 else (slice(None), slice(None))
            loads.append(pltpu.make_async_copy(a.at[at], held.at[at], refs[12].at[len(loads)]))
            stores.append(pltpu.make_async_copy(held.at[at], b.at[at], refs[13].at[len(stores)]))
    for cp in loads:
        cp.start()
    for load, cp in zip(loads, stores):
        load.wait()
        cp.start()
    for cp in stores:
        cp.wait()


def per_device(tokens, routes, gates, out_grad, gate_weight, up_weight, down_weight):
    results = main_call(tokens, routes, gates, out_grad, gate_weight, up_weight, down_weight)
    hbm = pl.BlockSpec(memory_space=pl.ANY)
    return pl.pallas_call(
        copy_kernel,
        out_shape=tuple(jax.ShapeDtypeStruct(a.shape, a.dtype) for a in results),
        in_specs=[hbm] * 4,
        out_specs=(hbm,) * 4,
        scratch_shapes=[pltpu.VMEM(a.shape, a.dtype) for a in results] + [pltpu.SemaphoreType.DMA((13,))] * 2,
        name="copy_results",
    )(*results)


def solution(mesh):
    return jax.shard_map(
        per_device,
        mesh=mesh,
        in_specs=(
            P(("expert", "fsdp"), None),
            P(("expert", "fsdp"), None),
            P(("expert", "fsdp"), None),
            P(("expert", "fsdp"), None),
            P("expert", None, "fsdp"),
            P("expert", None, "fsdp"),
            P("expert", "fsdp", None),
        ),
        out_specs=(
            P(("expert", "fsdp"), None),
            P("expert", None, "fsdp"),
            P("expert", None, "fsdp"),
            P("expert", "fsdp", None),
        ),
        check_vma=False,
    )
```

time: 93 us -> 84.8 us (0.912)
  matrix products: 10.2 us -> 0 us
  Pallas kernels: 80.9 us -> 83.7 us
  local copies, waits for them, and re-layouts: 1.03 us -> 0 us
    dot_general x3 -> x0, matrix products: 10.2 us -> none  [contract_rows(): lax.dot_general(left, right, (((0,), (0,)), ((), ())), preferred_element_...]
    pallas_call x0 -> x1, Pallas kernels: none -> 5.5 us  [per_device(): pl.pallas_call(copy_kernel, out_shape=tuple((jax.ShapeDtypeStruct(a.shape...]
    pallas_call x1, Pallas kernels: 80.9 us -> 78.2 us  [main_call(): pl.pallas_call(main_kernel, out_shape=(jax.ShapeDtypeStruct((2, D), BF),...]
    unnamed x9 -> x0, local copies, waits for them, and re-layouts: 1.03 us -> none
where the time goes in v3:
time: 84.8 us; the launch traced here: 84.5 us
  Pallas kernels  83.7 us (99%)
    pallas_call x1, Pallas kernels, main_call(): pl.pallas_call(main_kernel, out_shape=(jax.ShapeDtypeStruct((2, D), BF),...  78.2 us
    pallas_call x1, Pallas kernels, per_device(): pl.pallas_call(copy_kernel, out_shape=tuple((jax.ShapeDtypeStruct(a.shape...  5.5 us

profile of v3, /device:TPU:1, one launch (start us, length us, event | category | flops | bytes accessed | tf_op | source)
XLA Modules:
  0.0 84.5 jit_solution(16199573249091957199)
XLA Ops:
  0.6 78.2 %gather_compute_sum.1 = (bf16[2,4096]{1,0:T(2,128)(2,1)}, bf16[1,4096,256]{2,1,0:T(8,128)(2,1)}, bf16[1,4096,256]{2,1,0:T(8,128)(2,1)}, bf16[1,256,4096]{2,1,0:T(8,128)(2,1)}) custom-call(bf16[2,4096]{1,0:T(2,128)(2,1)} %tok_ref.1, s32[2,2]{1,0:T(2,128)} %route_ref.1, f32[2,2]{1,0:T(2,128)} %gate_ref.1, bf16[2,4096]{1,0:T(2,128)(2,1)} %og_ref.1, ...), custom_call_target="tpu_custom_call" | custom-call | tf_op jit(solution)/shard_map/gather_compute_sum/pallas_call | solution.py:466
  78.9 5.5 %copy_results.1 = (bf16[2,4096]{1,0:T(2,128)(2,1)}, bf16[1,4096,256]{2,1,0:T(8,128)(2,1)}, bf16[1,4096,256]{2,1,0:T(8,128)(2,1)}, bf16[1,256,4096]{2,1,0:T(8,128)(2,1)}) custom-call(bf16[2,4096]{1,0:T(2,128)(2,1)} %get-tuple-element.8.refs_0_, bf16[1,4096,256]{2,1,0:T(8,128)(2,1)} %get-tuple-element.9.refs_1_, ...), custom_call_target="tpu_custom_call" | custom-call | tf_op jit(solution)/shard_map/copy_results/pallas_call | solution.py:519

commit v4 on v3

--- a/solution.py
+++ b/solution.py
@@ -31,11 +31,11 @@
 
 
 def main_kernel(
-    tok_ref, route_ref, gate_ref, og_ref, wg_hbm, wu_hbm, wd_hbm,
+    tok_hbm, route_hbm, gate_hbm, og_hbm, wg_hbm, wu_hbm, wd_hbm,
     out, dwg_hbm, dwu_hbm, dwd_hbm,
-    big, stk, zbuf, blk, wg, wu, wd, act, gu, hs, hst, dwg, dwu, dwd,
-    pgo, sbuf, far, far_in, near, kept, joined, own1, r1, acc1, r2, own2, zs, r3,
-    wsem, osem, s1, rv1, sp, rp, sa, ra, sb, rb, sf, rf, szp, rzp, szm, rzm, ssib, rsib,
+    route_ref, gate_ref, big, stk, zbuf, blk, wg, wu, wd, act, gu, hs, hst, dwg, dwu, dwd,
+    pgo, sbuf, far, far_in, last_in, last_near, near, kept, joined, own1, r1, acc1, r2, own2, zs, r3,
+    isem, wsem, osem, s1, rv1, sp, rp, sa, ra, rb, rf, sz, rzp, rzm, ssib, rsib,
     ss0, rs0, ss1, rs1, ss2, rs2, ss3, rs3,
 ):
     e = lax.axis_index("expert")
@@ -72,13 +72,23 @@
             src_ref=src, dst_ref=dst, send_sem=ss, recv_sem=rs, device_id=d, device_id_type=MESH
         )
 
-    sends = []
-
     def go(*args):
-        cp = rc(*args)
+        rc(*args).start()
+
+    def sent(ref, sem):
+        rc(ref, ref, sem, sem, sib).wait_send()
+
+    def came(ref, sem):
+        rc(ref, ref, sem, sem, sib).wait_recv()
+
+    inputs = [
+        pltpu.make_async_copy(route_hbm, route_ref, isem.at[0]),
+        pltpu.make_async_copy(gate_hbm, gate_ref, isem.at[1]),
+        pltpu.make_async_copy(tok_hbm, stk.at[0, :, 0:D], isem.at[2]),
+        pltpu.make_async_copy(og_hbm, stk.at[1, :, 0:D], isem.at[3]),
+    ]
+    for cp in inputs:
         cp.start()
-        sends.append(cp)
-
     bar = pltpu.get_barrier_semaphore()
     zoff = [(dd, cc) for dd in range(8) for cc in range(2) if (dd, cc) != (0, 0)]
     poff = [(a, b) for a in range(4) for b in range(4) if (a, b) != (0, 0)]
@@ -93,8 +103,8 @@
     ]
     for cp in loads:
         cp.start()
-    stk[0, :, 0:D] = tok_ref[...]
-    stk[1, :, 0:D] = og_ref[...]
+    for cp in inputs:
+        cp.wait()
     lane = lax.broadcasted_iota(jnp.int32, (2, 128), 1)
     dense = jnp.zeros((2, 128), F32)
     for k in range(2):
@@ -114,7 +124,7 @@
         for i in order:
             dd, cc = zoff[i]
             go(
-                stk.at[core[cc], :, lo:hi], zbuf.at[me, :, lo:hi], s1.at[15 * t + i], rv1.at[15 * t + i], dz(dd, cc)
+                stk.at[core[cc], :, lo:hi], zbuf.at[me, :, lo:hi], s1.at[t], rv1.at[t], dz(dd, cc)
             )
     zbuf[me] = stk[c]
     jo = bj(0, 0)
@@ -122,10 +132,7 @@
 
     def take_line(t):
         lo, hi = line[t]
-        for i in reversed(order):
-            dd, cc = zoff[i]
-            src = zz[(8 - dd) % 8] * 2 + core[cc]
-            rc(stk.at[0, :, lo:hi], zbuf.at[src, :, lo:hi], s1.at[15 * t + i], rv1.at[15 * t + i], sib).wait_recv()
+        came(zbuf.at[0:15, :, lo:hi], rv1.at[t])
         for i in range(16):
             blk[2 * i : 2 * i + 2, lo:hi] = zbuf[i, :, lo:hi].astype(F32)
         if t == 0:
@@ -146,36 +153,28 @@
         j = gj(g, a, 0)
         for t, s in ((0, 1), (1, 3)):
             i = 8 * g + 2 * k + t
-            go(part(g, j), part(g, j), sb.at[i], rb.at[i], gdv(g, 0, s))
-
-    arrivals = {}
-
-    def sibsend(key, ref, oref=None):
-        i = len(arrivals)
-        go(ref, ref, ssib.at[i], rsib.at[i], sib)
-        if oref is None:
-            g, a, b = key
-            oref = big.at[c0, gj(g, b, a), :, SEG[g][0] : SEG[g][1]]
-        arrivals[key] = (oref, i)
-
-    def sibwait(key):
-        oref, i = arrivals[key]
-        rc(oref, oref, ssib.at[i], rsib.at[i], sib).wait_recv()
+            go(part(g, j), part(g, j), sa.at[g], rb.at[i], gdv(g, 0, s))
+
+    def group(g, a):
+        return 2 * g + (1 if a in (1, 2) else 0)
+
+    def sibsend(g, a, ref):
+        go(ref, ref, ssib, rsib.at[group(g, a)], sib)
 
     def own_send(g):
         for a in (1, 3, 2):
             i = 3 * g + a - 1
-            go(part(g, jo), part(g, jo), sa.at[i], ra.at[i], gdv(g, a, 0))
+            go(part(g, jo), part(g, jo), sa.at[g], ra.at[i], gdv(g, a, 0))
         a2send(g, 0, 0)
-        sibsend((g, 0, 0), part(g, jo))
+        sibsend(g, 0, part(g, jo))
 
     def a1recv(g):
         for a in (1, 3, 2):
             j = gj(g, 4 - a, 0)
             i = 3 * g + a - 1
-            rc(part(g, jo), part(g, j), sa.at[i], ra.at[i], sib).wait_recv()
+            came(part(g, j), ra.at[i])
             a2send(g, a, 4 - a)
-            sibsend((g, 4 - a, 0), part(g, j))
+            sibsend(g, 4 - a, part(g, j))
 
     def half(g, j, h):
         return big.at[c, j, 16 * h : 16 * h + 16, SEG[g][0] : SEG[g][1]]
@@ -186,17 +185,15 @@
         for h, b in ((0, 3), (1, 1)):
             j = gj(g, a, b)
             i = 8 * g + 2 * slot[a] + h
-            rc(part(g, jo), part(g, j), sb.at[i], rb.at[i], sib).wait_recv()
-            go(half(g, j, h), half(g, j, h), sf.at[i], rf.at[i], gdv(g, 0, 4 - b))
+            came(part(g, j), rb.at[i])
+            go(half(g, j, h), half(g, j, h), sa.at[g], rf.at[4 * g + slot[a]], gdv(g, 0, 4 - b))
         for b in (3, 1):
-            sibsend((g, a, b), part(g, gj(g, a, b)))
+            sibsend(g, a, part(g, gj(g, a, b)))
 
     def a2fin(g, a):
         j = gj(g, a, 2)
-        for h in range(2):
-            i = 8 * g + 2 * slot[a] + h
-            rc(half(g, jo, h), half(g, j, h), sf.at[i], rf.at[i], sib).wait_recv()
-        sibsend((g, a, 2), part(g, j))
+        came(part(g, j), rf.at[4 * g + slot[a]])
+        sibsend(g, a, part(g, j))
 
     def zc(k):
         return pl.ds(pl.multiple_of(SL * zz[k % 8], 128), SL)
@@ -208,20 +205,20 @@
     def zsend(h, u):
         i = SUB * h + u
         if h < 3 or u < SUB // 2:
-            go(piece(-h, u), piece(-h, u), szp.at[i], rzp.at[i], dz(1, 0))
+            go(piece(-h, u), piece(-h, u), sz, rzp.at[i], dz(1, 0))
         if h < 3 or u >= SUB // 2:
-            go(piece(h, u), piece(h, u), szm.at[i], rzm.at[i], dz(7, 0))
+            go(piece(h, u), piece(h, u), sz, rzm.at[i], dz(7, 0))
 
     def zsib(k):
-        sibsend(("z", k), big.at[c, :, :, zc(k)], big.at[c0, :, :, zc(k)])
+        go(big.at[c, :, :, zc(k)], big.at[c, :, :, zc(k)], ssib, rsib.at[4], sib)
 
     def zrecv(h):
         for u in range(SUB):
             i = SUB * h + u
             if h < 3 or u < SUB // 2:
-                rc(piece(0, u), piece(-h - 1, u), szp.at[i], rzp.at[i], sib).wait_recv()
+                came(piece(-h - 1, u), rzp.at[i])
             if h < 3 or u >= SUB // 2:
-                rc(piece(0, u), piece(h + 1, u), szm.at[i], rzm.at[i], sib).wait_recv()
+                came(piece(h + 1, u), rzm.at[i])
             if h < 3:
                 zsend(h + 1, u)
         zsib(-h - 1)
@@ -229,13 +226,12 @@
             zsib(h + 1)
 
     take_line(0)
-    for i, (a, b) in enumerate(poff):
-        go(big.at[c, jo, :, mycol], big.at[c, jo, :, mycol], sp.at[i], rp.at[i], dv(a, b))
+    for a, b in poff:
+        go(big.at[c, jo, :, mycol], big.at[c, jo, :, mycol], sp, rp, dv(a, b))
     own_send(0)
     take_line(1)
     own_send(1)
-    for i, (a, b) in enumerate(poff):
-        rc(big.at[c, jo, :, mycol], big.at[c, bj(4 - a, 4 - b), :, mycol], sp.at[i], rp.at[i], sib).wait_recv()
+    came(big.at[c, 0:15, :, mycol], rp)
     for u in range(SUB):
         zsend(0, u)
     zsib(0)
@@ -256,9 +252,7 @@
                 act[t, n, j] = val[32 * i : 32 * i + 32]
 
     def acts_a(g, offsets):
-        for a in offsets:
-            for b in range(4):
-                sibwait((g, a, b))
+        came(big.at[c0, 0:8, :, SEG[g][0] : SEG[g][1]], rsib.at[group(g, offsets[0])])
         for arr in (0, 1):
             acts(g, arr, [j for a in offsets for j in rows_of(arr ^ g, a)], *DATA[g])
 
@@ -289,8 +283,7 @@
     acts_a(0, (1, 2))
     a2fin(1, 2)
     acts_a(1, (0, 3))
-    for k in range(-4, 4):
-        sibwait(("z", k))
+    came(big.at[c0, :, :, 0:CB], rsib.at[4])
     for arr in (0, 1):
         acts(2, arr, list(range(16)), 0, CB)
     acts_a(1, (1, 2))
@@ -318,13 +311,9 @@
         return 0
 
     lax.fori_loop(0, 4, hidden_rows, 0)
-    save = []
-
     def store(refs):
-        for a, b in refs:
-            cp = pltpu.make_async_copy(a, b, osem.at[len(save)])
-            cp.start()
-            save.append(cp)
+        for n, (a, b) in enumerate(refs):
+            pltpu.make_async_copy(a, b, osem.at[n]).start()
 
     def weight_grads(t):
         cols = slice(512 * t, 512 * t + 512)
@@ -358,50 +347,55 @@
 
     def sum_send(q):
         val = share(q, c).reshape(16, 32, QC)
-        rc(pgo.at[q], sbuf.at[q], ss0.at[q], rs0.at[q], sib).wait_recv()
+        rc(pgo.at[q], sbuf.at[q], ss0, rs0.at[q], sib).wait_recv()
 
         def at(a, b):
             return val[b * 4 + a] + sbuf[q, a * 4 + b].astype(F32)
 
         for a in range(4):
             far[q, a] = at(a, 2).astype(BF)
+        if q == NQ - 1:
+            go(far.at[q], last_in, ss1, rs1.at[2 * q], sdv(q, 0, 2))
+            for h, b in ((0, 1), (1, 3)):
+                for a in range(4):
+                    last_near[h, a] = at(a, b).astype(BF)
+                go(last_near.at[h], r1.at[q, h], ss1, rs1.at[2 * q + 1], sdv(q, 0, b))
+            for a in range(4):
+                own1[q, a] = at(a, 0)
+            return
         for h, b in ((0, 1), (1, 3)):
-            i = 6 * q + h
-            go(far.at[q, 2 * h : 2 * h + 2], far_in.at[q, h], ss1.at[i], rs1.at[i], sdv(q, 0, b))
+            go(far.at[q, 2 * h : 2 * h + 2], far_in.at[q, h], ss1, rs1.at[2 * q], sdv(q, 0, b))
         for h, b in ((0, 1), (1, 3)):
-            i = 6 * q + 2 + h
             for a in range(2):
                 near[q, h, a] = at(2 - 2 * h + a, b).astype(BF)
                 kept[q, h, a] = at(2 * h + a, b)
-            go(near.at[q, h], r1.at[q, h, 2 - 2 * h : 4 - 2 * h], ss1.at[i], rs1.at[i], sdv(q, 0, b))
+            go(near.at[q, h], r1.at[q, h, 2 - 2 * h : 4 - 2 * h], ss1, rs1.at[2 * q + 1], sdv(q, 0, b))
         for a in range(4):
             own1[q, a] = at(a, 0)
 
     def join(q):
+        came(far_in.at[q], rs1.at[2 * q])
         for h, b in ((0, 1), (1, 3)):
-            i = 6 * q + h
-            rc(far.at[q, 0:2], far_in.at[q, h], ss1.at[i], rs1.at[i], sib).wait_recv()
             joined[q, h] = (kept[q, h] + far_in[q, h].astype(F32)).astype(BF)
-            i = 6 * q + 4 + h
-            go(joined.at[q, h], r1.at[q, h, 2 * h : 2 * h + 2], ss1.at[i], rs1.at[i], sdv(q, 0, b))
+            go(joined.at[q, h], r1.at[q, h, 2 * h : 2 * h + 2], ss1, rs1.at[2 * q + 1], sdv(q, 0, b))
 
     def second(q):
-        for h in range(2):
-            for i, lo in ((6 * q + 2 + h, 2 - 2 * h), (6 * q + 4 + h, 2 * h)):
-                rc(near.at[q, h], r1.at[q, h, lo : lo + 2], ss1.at[i], rs1.at[i], sib).wait_recv()
+        last = q == NQ - 1
+        if last:
+            came(last_in, rs1.at[2 * q])
+        came(r1.at[q], rs1.at[2 * q + 1])
         for a in (2, 1, 3, 0):
             s = own1[q, a] + r1[q, 0, a].astype(F32) + r1[q, 1, a].astype(F32)
+            if last:
+                s = s + last_in[a].astype(F32)
             if a:
-                i = q * 3 + a - 1
                 acc1[q, a - 1] = s.astype(BF)
-                go(acc1.at[q, a - 1], r2.at[q, a - 1], ss2.at[i], rs2.at[i], sdv(q, a, 0))
+                go(acc1.at[q, a - 1], r2.at[q, a - 1], ss2, rs2.at[q], sdv(q, a, 0))
             else:
                 own2[q] = s
 
     def third(q):
-        for a in (1, 3, 2):
-            i = q * 3 + a - 1
-            rc(acc1.at[q, a - 1], r2.at[q, a - 1], ss2.at[i], rs2.at[i], sib).wait_recv()
+        came(r2.at[q], rs2.at[q])
         own2[q] = own2[q] + r2[q, 0].astype(F32) + r2[q, 1].astype(F32) + r2[q, 2].astype(F32)
         for i in range(16):
             zs[q // 2, i, :, q % 2 * QC : q % 2 * QC + QC] = own2[q, 2 * i : 2 * i + 2, :].astype(BF)
@@ -409,29 +403,33 @@
     def line_send(t):
         for i in order:
             dd, cc = zoff[i]
-            go(zs.at[t, zz[dd] * 2 + core[cc]], r3.at[t, z, c], ss3.at[15 * t + i], rs3.at[15 * t + i], dz(dd, cc))
+            go(zs.at[t, zz[dd] * 2 + core[cc]], r3.at[t, z, c], ss3.at[t], rs3.at[t], dz(dd, cc))
         r3[t, z, c] = zs[t, me]
 
     def line_sum(t):
-        for i in reversed(order):
-            dd, cc = zoff[i]
-            here = r3.at[t, zz[(8 - dd) % 8], core[cc]]
-            rc(zs.at[t, 0], here, ss3.at[15 * t + i], rs3.at[15 * t + i], sib).wait_recv()
+        came(zs.at[t, 0:15], rs3.at[t])
         for h in range(2):
             s = r3[t, 0, h].astype(F32)
             for k in range(1, 8):
                 s = s + r3[t, k, h].astype(F32)
             out[:, h * HW + t * HW // 2 : h * HW + (t + 1) * HW // 2] = s.astype(BF)
 
-    for q in range(NQ):
+    def other_half(q):
         pgo[q] = share(q, c0).astype(BF).reshape(16, 32, QC)
-        go(pgo.at[q], sbuf.at[q], ss0.at[q], rs0.at[q], sib)
-    for q in range(NQ):
-        sum_send(q)
-        if q:
-            join(q - 1)
+        go(pgo.at[q], sbuf.at[q], ss0, rs0.at[q], sib)
+
+    other_half(0)
+    other_half(1)
+    sum_send(0)
+    other_half(2)
+    sum_send(1)
+    other_half(3)
+    join(0)
+    sum_send(2)
+    join(1)
+    sum_send(3)
     hst[...] = hs[...].reshape(512, FB).astype(F32).T.astype(BF)
-    join(NQ - 1)
+    join(2)
     weight_grads(0)
     second(0)
     weight_grads(1)
@@ -439,10 +437,10 @@
     weight_grads(2)
     second(2)
     weight_grads(3)
-    second(3)
     third(0)
     third(1)
     line_send(0)
+    second(3)
     weight_grads(4)
     third(2)
     third(3)
@@ -452,10 +450,19 @@
     weight_grads(7)
     line_sum(0)
     line_sum(1)
-    for cp in sends:
-        cp.wait_send()
-    for cp in save:
-        cp.wait()
+    for t, (lo, hi) in enumerate(line):
+        sent(zbuf.at[0:15, :, lo:hi], s1.at[t])
+        sent(zs.at[t, 0:15], ss3.at[t])
+    sent(big.at[c, 0:15, :, mycol], sp)
+    for g, (lo, hi) in enumerate(SEG):
+        sent(big.at[c, 0:15, :, lo:hi], sa.at[g])
+    sent(big.at[c, :, :, 0 : 7 * SL], sz)
+    sent(big.at[c], ssib)
+    sent(pgo, ss0)
+    sent(pgo.at[0:3], ss1)
+    sent(pgo.at[0, 0:12], ss2)
+    for n, (a, b) in enumerate(((dwg, dwg_hbm), (dwu, dwu_hbm), (dwd, dwd_hbm))):
+        pltpu.make_async_copy(a, b.at[0], osem.at[n]).wait()
 
 
 def main_call(*args):
@@ -471,22 +478,21 @@
             jax.ShapeDtypeStruct((1, D, FB), BF),
             jax.ShapeDtypeStruct((1, FB, D), BF),
         ),
-        in_specs=[vm, vm, vm, vm, hbm, hbm, hbm],
+        in_specs=[hbm] * 7,
         out_specs=(vm, hbm, hbm, hbm),
         scratch_shapes=[
-            V((2, 16, 32, W), BF), V((2, 2, W), BF), V((16, 2, W), BF), V((32, W), F32),
+            V((2, 2), jnp.int32), V((2, 2), F32), V((2, 16, 32, W), BF), V((2, 2, W), BF), V((16, 2, W), BF), V((32, W), F32),
             V((D, FB), BF), V((D, FB), BF), V((FB, D), BF),
             V((3, 3, 16, 32, FB), F32),
             V((16, 32, 2 * FB), BF), V((16, 32, FB), BF), V((FB, 512), BF),
             V((D, FB), BF), V((D, FB), BF), V((FB, D), BF),
-            V((NQ, 16, 32, QC), BF), V((NQ, 16, 32, QC), BF), V((NQ, 4, 32, QC), BF), V((NQ, 2, 2, 32, QC), BF),
+            V((NQ, 16, 32, QC), BF), V((NQ, 16, 32, QC), BF), V((NQ, 4, 32, QC), BF), V((NQ, 2, 2, 32, QC), BF), V((4, 32, QC), BF), V((2, 4, 32, QC), BF),
             V((NQ, 2, 2, 32, QC), BF), V((NQ, 2, 2, 32, QC), F32), V((NQ, 2, 2, 32, QC), BF), V((NQ, 4, 32, QC), F32),
             V((NQ, 2, 4, 32, QC), BF), V((NQ, 3, 32, QC), BF), V((NQ, 3, 32, QC), BF), V((NQ, 32, QC), F32),
             V((2, 16, 2, HW // 2), BF), V((2, 8, 2, 2, HW // 2), BF),
-            dma((3,)), dma((24,)), dma((30,)), dma((30,)), dma((15,)), dma((15,)), dma((6,)), dma((6,)),
-            dma((16,)), dma((16,)), dma((16,)), dma((16,)), dma((4 * SUB,)), dma((4 * SUB,)), dma((4 * SUB,)), dma((4 * SUB,)),
-            dma((40,)), dma((40,)), dma((NQ,)), dma((NQ,)), dma((6 * NQ,)), dma((6 * NQ,)),
-            dma((3 * NQ,)), dma((3 * NQ,)), dma((30,)), dma((30,)),
+            dma((4,)), dma((3,)), dma((3,)), dma((2,)), dma((2,)), dma, dma, dma((2,)), dma((6,)), dma((16,)), dma((8,)),
+            dma, dma((4 * SUB,)), dma((4 * SUB,)), dma, dma((5,)), dma, dma((NQ,)), dma, dma((2 * NQ,)),
+            dma, dma((NQ,)), dma((2,)), dma((2,)),
         ],
         compiler_params=pltpu.CompilerParams(
             collective_id=0, has_side_effects=True, vmem_limit_bytes=60 << 20

time: 84.8 us -> 80.2 us (0.946)
  Pallas kernels: 83.7 us -> 79.2 us
    pallas_call x1, Pallas kernels: 78.2 us -> 73.7 us  [main_call(): pl.pallas_call(main_kernel, out_shape=(jax.ShapeDtypeStruct((2, D), BF),...]
where the time goes in v4:
time: 80.2 us; the launch traced here: 80 us
  Pallas kernels  79.2 us (99%)
    pallas_call x1, Pallas kernels, main_call(): pl.pallas_call(main_kernel, out_shape=(jax.ShapeDtypeStruct((2, D), BF),...  73.7 us
    pallas_call x1, Pallas kernels, per_device(): pl.pallas_call(copy_kernel, out_shape=tuple((jax.ShapeDtypeStruct(a.shape...  5.5 us

profile of v4, /device:TPU:1, one launch (start us, length us, event | category | flops | bytes accessed | tf_op | source)
XLA Modules:
  0.0 80.0 jit_solution(4922666545981819179)
XLA Ops:
  0.6 73.7 %gather_compute_sum.1 = (bf16[2,4096]{1,0:T(2,128)(2,1)}, bf16[1,4096,256]{2,1,0:T(8,128)(2,1)}, bf16[1,4096,256]{2,1,0:T(8,128)(2,1)}, bf16[1,256,4096]{2,1,0:T(8,128)(2,1)}) custom-call(bf16[2,4096]{1,0:T(2,128)(2,1)} %tok_hbm.1, s32[2,2]{1,0:T(2,128)} %route_hbm.1, f32[2,2]{1,0:T(2,128)} %gate_hbm.1, bf16[2,4096]{1,0:T(2,128)(2,1)} %og_hbm.1, ...), custom_call_target="tpu_custom_call" | custom-call | tf_op jit(solution)/shard_map/gather_compute_sum/pallas_call | solution.py:473
  74.4 5.5 %copy_results.1 = (bf16[2,4096]{1,0:T(2,128)(2,1)}, bf16[1,4096,256]{2,1,0:T(8,128)(2,1)}, bf16[1,4096,256]{2,1,0:T(8,128)(2,1)}, bf16[1,256,4096]{2,1,0:T(8,128)(2,1)}) custom-call(bf16[2,4096]{1,0:T(2,128)(2,1)} %get-tuple-element.8.refs_0_, bf16[1,4096,256]{2,1,0:T(8,128)(2,1)} %get-tuple-element.9.refs_1_, ...), custom_call_target="tpu_custom_call" | custom-call | tf_op jit(solution)/shard_map/copy_results/pallas_call | solution.py:525

commit v5 on v4

--- a/solution.py
+++ b/solution.py
@@ -281,11 +281,11 @@
     a2fin(1, 3)
     a2fin(1, 1)
     acts_a(0, (1, 2))
-    a2fin(1, 2)
-    acts_a(1, (0, 3))
     came(big.at[c0, :, :, 0:CB], rsib.at[4])
     for arr in (0, 1):
         acts(2, arr, list(range(16)), 0, CB)
+    a2fin(1, 2)
+    acts_a(1, (0, 3))
     acts_a(1, (1, 2))
 
     lane32 = lax.broadcasted_iota(jnp.int32, (128, 128), 1)
@@ -504,7 +504,7 @@
 def copy_kernel(*refs):
     loads, stores = [], []
     for a, b, held in zip(refs[0:4], refs[4:8], refs[8:12]):
-        pieces = 4 if a.shape[0] == 1 else 1
+        pieces = 8 if a.shape[0] == 1 else 1
         n = a.shape[1] // pieces
         for i in range(pieces):
             at = (slice(None), slice(n * i, n * i + n)) if pieces > 1 else (slice(None), slice(None))
@@ -527,7 +527,7 @@
         out_shape=tuple(jax.ShapeDtypeStruct(a.shape, a.dtype) for a in results),
         in_specs=[hbm] * 4,
         out_specs=(hbm,) * 4,
-        scratch_shapes=[pltpu.VMEM(a.shape, a.dtype) for a in results] + [pltpu.SemaphoreType.DMA((13,))] * 2,
+        scratch_shapes=[pltpu.VMEM(a.shape, a.dtype) for a in results] + [pltpu.SemaphoreType.DMA((25,))] * 2,
         name="copy_results",
     )(*results)
 

time: 80.2 us -> 80.2 us (level)
  no operation moved by 1% of the time
where the time goes in v5:
time: 80.2 us; the launch traced here: 80 us
  Pallas kernels  79.2 us (99%)
    pallas_call x1, Pallas kernels, main_call(): pl.pallas_call(main_kernel, out_shape=(jax.ShapeDtypeStruct((2, D), BF),...  73.6 us
    pallas_call x1, Pallas kernels, per_device(): pl.pallas_call(copy_kernel, out_shape=tuple((jax.ShapeDtypeStruct(a.shape...  5.59 us

profile of v5, /device:TPU:1, one launch (start us, length us, event | category | flops | bytes accessed | tf_op | source)
XLA Modules:
  0.0 80.0 jit_solution(4186028477944419893)
XLA Ops:
  0.6 73.6 %gather_compute_sum.1 = (bf16[2,4096]{1,0:T(2,128)(2,1)}, bf16[1,4096,256]{2,1,0:T(8,128)(2,1)}, bf16[1,4096,256]{2,1,0:T(8,128)(2,1)}, bf16[1,256,4096]{2,1,0:T(8,128)(2,1)}) custom-call(bf16[2,4096]{1,0:T(2,128)(2,1)} %tok_hbm.1, s32[2,2]{1,0:T(2,128)} %route_hbm.1, f32[2,2]{1,0:T(2,128)} %gate_hbm.1, bf16[2,4096]{1,0:T(2,128)(2,1)} %og_hbm.1, ...), custom_call_target="tpu_custom_call" | custom-call | tf_op jit(solution)/shard_map/gather_compute_sum/pallas_call | solution.py:473
  74.2 5.6 %copy_results.1 = (bf16[2,4096]{1,0:T(2,128)(2,1)}, bf16[1,4096,256]{2,1,0:T(8,128)(2,1)}, bf16[1,4096,256]{2,1,0:T(8,128)(2,1)}, bf16[1,256,4096]{2,1,0:T(8,128)(2,1)}) custom-call(bf16[2,4096]{1,0:T(2,128)(2,1)} %get-tuple-element.8.refs_0_, bf16[1,4096,256]{2,1,0:T(8,128)(2,1)} %get-tuple-element.9.refs_1_, ...), custom_call_target="tpu_custom_call" | custom-call | tf_op jit(solution)/shard_map/copy_results/pallas_call | solution.py:525
